TPU v7x, 32 devices: a whole 2x2x4 slice. The times are simulated.
32 devices in a mesh: groups: 2 (over y), seq: 4 (over z), sub: 2 (over x), rep: 2 (over core).
Axes of the slice: x: 2, y: 2, z: 4, core: 2. Of those that a mesh axis runs over, the one named last changes fastest.
Arguments:
- moe_input: bfloat16 [2048, 2048], P(('groups', 'seq'), ('sub', 'rep')), parts along dimension 0, may hold values from -6 to 6
- upstream: bfloat16 [2048, 2048], P(('groups', 'seq'), ('sub', 'rep')), parts along dimension 0, may hold values from -6 to 6
- expert_ids: int32 [2048, 2], P(('groups', 'seq')), parts along dimension 0, may hold values from 0 to 7, all different within a row; in each aligned block of 256 rows (0 to 255, 256 to 511, ...) at most 96 rows name the same one
- router_weight: float32 [2048, 2], P(('groups', 'seq')), parts along dimension 0, may hold values from 0.05 to 1
- w_gate: bfloat16 [8, 2048, 768], P('seq', ('sub', 'rep')), may hold values from -0.125 to 0.125
- w_up: bfloat16 [8, 2048, 768], P('seq', ('sub', 'rep')), may hold values from -0.125 to 0.125
- w_down: bfloat16 [8, 768, 2048], P('seq', None, ('sub', 'rep')), may hold values from -0.21875 to 0.21875
- out_proj: bfloat16 [2048, 2048], P(('sub', 'rep')), may hold values from -0.125 to 0.125
- query: bfloat16 [2048, 2048], P(('groups', 'seq'), ('sub', 'rep')), parts along dimension 0, may hold values from -8 to 8
- key_in: bfloat16 [2048, 2048], P(('groups', 'seq'), ('sub', 'rep')), parts along dimension 0, may hold values from -8 to 8
- value: bfloat16 [2048, 2048], P(('groups', 'seq'), ('sub', 'rep')), parts along dimension 0, may hold values from -6 to 6
Outputs:
- resid_grad: bfloat16 [2048, 2048], P(('groups', 'seq'), ('sub', 'rep')), parts along dimension 0
- query_grad: bfloat16 [2048, 2048], P(('groups', 'seq'), ('sub', 'rep')), parts along dimension 0
- key_grad: bfloat16 [2048, 2048], P(('groups', 'seq'), ('sub', 'rep')), parts along dimension 0
- value_grad: bfloat16 [2048, 2048], P(('groups', 'seq'), ('sub', 'rep')), parts along dimension 0
There are 2 independent parts, one for each index of `groups`. A program takes and returns all parts, laid end to end along the dimension named above; an argument that names none is the same for every part. Nothing has to cross between parts.
Inputs may be any that keep to these rules, and one draw needn't show every extreme that they name: `expert_ids`: each row names two different experts. In each aligned block of 256 rows (the rows of one index of seq) no expert is named by more than 96 rows, a bound that some block reaches.
All inputs are finite; a program needn't handle non-finite values.
Results may differ from a plain program's by a relative error of at most 0.02.
Values may be sent and summed in bfloat16 or wider, within the bound.
A program may use at most 64 MiB of HBM per device.

v0:
```python
import jax
import jax.numpy as jnp
from jax import lax
from jax.sharding import PartitionSpec as P

HEAD_DIM = 128
WINDOW = 128


def entering(shard, axis, combine, identity, reverse):
    length, index = (lax.axis_size(axis), lax.axis_index(axis))
    everything = lax.all_gather(shard.astype(jnp.bfloat16), axis)
    start = jnp.broadcast_to(jnp.asarray(identity, shard.dtype), shard.shape)

    def step(k, before):
        at = length - 1 - k if reverse else k
        reached = at > index if reverse else at < index
        new = combine(before, everything[at].astype(shard.dtype))
        return jnp.where(reached, new, before)

    return lax.fori_loop(0, length, step, start)


def shifted(block, axis, distance):
    devices = range(lax.axis_size(axis))
    route = [(i - distance, i) for i in devices if i - distance in devices]
    return lax.ppermute(block, axis, route)


def add_single(before_part, after_part):
    return before_part + after_part


def silu_grads(pre_gate, pre_up, hidden_grad):
    sigmoid_gate = jax.nn.sigmoid(pre_gate)
    gate_grad = hidden_grad * pre_up * sigmoid_gate * (1.0 + pre_gate * (1.0 - sigmoid_gate))
    up_grad = hidden_grad * pre_gate * sigmoid_gate
    return (gate_grad.astype(jnp.bfloat16), up_grad.astype(jnp.bfloat16))


def window_block(query_heads, keys_ext, values_ext, grad_heads, first_key):
    row_count = query_heads.shape[0]
    key_count = keys_ext.shape[0]
    scaling = query_heads.shape[-1] ** (-0.5)
    query_pos = lax.broadcasted_iota(jnp.int32, (row_count, key_count), 0)
    key_pos = lax.broadcasted_iota(jnp.int32, (row_count, key_count), 1)
    allowed = (key_pos > query_pos) & (key_pos <= query_pos + WINDOW) & (key_pos + first_key >= 0)
    scores = (
        jnp.einsum("ihd,jhd->hij", query_heads, keys_ext, preferred_element_type=jnp.float32)
        * scaling
    )
    scores = jnp.where(allowed[None], scores, -jnp.inf)
    highest = jnp.max(scores, axis=2, keepdims=True)
    weights = jnp.exp(scores - highest)
    softmax_probs = weights / jnp.sum(weights, axis=2, keepdims=True)
    probs_low = softmax_probs.astype(jnp.bfloat16)
    attended = jnp.einsum("hij,jhe->ihe", probs_low, values_ext, preferred_element_type=jnp.float32)
    centre = jnp.sum(grad_heads.astype(jnp.float32) * attended, axis=2)
    prob_grad = jnp.einsum(
        "ihe,jhe->hij", grad_heads, values_ext, preferred_element_type=jnp.float32
    )
    score_grad = (softmax_probs * (prob_grad - jnp.transpose(centre)[:, :, None])).astype(
        jnp.bfloat16
    )
    win_query = (
        jnp.einsum("hij,jhd->ihd", score_grad, keys_ext, preferred_element_type=jnp.float32)
        * scaling
    )
    win_key = (
        jnp.einsum("hij,ihd->jhd", score_grad, query_heads, preferred_element_type=jnp.float32)
        * scaling
    )
    win_value = jnp.einsum(
        "hij,ihe->jhe", probs_low, grad_heads, preferred_element_type=jnp.float32
    )
    return (win_query, win_key, win_value)


def local(
    moe_input,
    upstream,
    expert_ids,
    router_weight,
    w_gate,
    w_up,
    w_down,
    out_proj,
    query,
    key_in,
    value,
):
    row_count, features = moe_input.shape
    seq_count = lax.axis_size("seq")
    local_experts = w_gate.shape[0]
    expert_count = local_experts * seq_count
    capacity = max(2, 3 * row_count // expert_count)
    chosen = expert_ids.shape[1]
    pair_ids = expert_ids.reshape(-1)
    pair_count = pair_ids.shape[0]
    one_hot = (pair_ids[:, None] == jnp.arange(expert_count, dtype=jnp.int32)[None, :]).astype(
        jnp.int32
    )
    slot_rank = jnp.sum((jnp.cumsum(one_hot, axis=0) - one_hot) * one_hot, axis=1)
    slot_index = pair_ids * capacity + slot_rank
    slot_owner = (
        jnp.zeros((expert_count * capacity,), jnp.int32)
        .at[slot_index]
        .set(jnp.arange(pair_count, dtype=jnp.int32) + 1)
    )
    live_slot = (slot_owner > 0)[:, None]
    token_row = jnp.maximum(slot_owner - 1, 0) // chosen
    slot_shape = (seq_count, local_experts, capacity, features)
    send_input = jnp.where(live_slot, moe_input[token_row], jnp.zeros((), jnp.bfloat16)).reshape(
        slot_shape
    )
    send_grad = jnp.where(live_slot, upstream[token_row], jnp.zeros((), jnp.bfloat16)).reshape(
        slot_shape
    )
    slot_input = lax.all_to_all(send_input, "seq", split_axis=0, concat_axis=0, tiled=True)
    slot_grad = lax.all_to_all(send_grad, "seq", split_axis=0, concat_axis=0, tiled=True)
    gate_part = jnp.einsum("nekf,efh->nekh", slot_input, w_gate, preferred_element_type=jnp.float32)
    up_part = jnp.einsum("nekf,efh->nekh", slot_input, w_up, preferred_element_type=jnp.float32)
    hidden_part = jnp.einsum(
        "nekf,ehf->nekh", slot_grad, w_down, preferred_element_type=jnp.float32
    )
    pre_gate = lax.psum(gate_part.astype(jnp.bfloat16), ("sub", "rep")).astype(jnp.float32)
    pre_up = lax.psum(up_part.astype(jnp.bfloat16), ("sub", "rep")).astype(jnp.float32)
    hidden_grad = lax.psum(hidden_part.astype(jnp.bfloat16), ("sub", "rep")).astype(jnp.float32)
    gate_grad, up_grad = silu_grads(pre_gate, pre_up, hidden_grad)
    input_grad = jnp.einsum("nekh,efh->nekf", gate_grad, w_gate, preferred_element_type=jnp.float32)
    input_grad = input_grad + jnp.einsum(
        "nekh,efh->nekf", up_grad, w_up, preferred_element_type=jnp.float32
    )
    expert_out = input_grad.astype(jnp.bfloat16)
    returned = lax.all_to_all(expert_out, "seq", split_axis=0, concat_axis=0, tiled=True).reshape(
        expert_count * capacity, features
    )
    pair_grads = returned[slot_index].astype(jnp.float32) * router_weight.reshape(-1)[:, None]
    combined = upstream.astype(jnp.float32) + jnp.sum(
        pair_grads.reshape(row_count, chosen, features), axis=1
    )
    resid_grad = combined.astype(jnp.bfloat16)
    head_grad = lax.dot_general(
        lax.all_gather(resid_grad, ("sub", "rep"), axis=1, tiled=True),
        out_proj,
        (((1,), (1,)), ((), ())),
        preferred_element_type=jnp.float32,
    ).astype(jnp.bfloat16)
    head_dim = HEAD_DIM
    local_heads = features // head_dim
    head_shape = (row_count, local_heads, head_dim)
    query_heads = query.reshape(head_shape)
    key_heads = key_in.reshape(head_shape)
    value_heads = value.reshape(head_shape)
    grad_heads = head_grad.reshape(head_shape)
    state_local = jnp.einsum(
        "shd,she->hde", key_heads, value_heads, preferred_element_type=jnp.float32
    )
    grad_local = jnp.einsum(
        "shd,she->hde", query_heads, grad_heads, preferred_element_type=jnp.float32
    )
    zero_state = jnp.zeros_like(state_local)
    preceding_state = entering(state_local, "seq", add_single, zero_state, False)
    gradient_following = entering(grad_local, "seq", add_single, zero_state, True)
    causal_masking = (
        lax.broadcasted_iota(jnp.int32, (row_count, row_count), 0)
        >= lax.broadcasted_iota(jnp.int32, (row_count, row_count), 1)
    )[None]
    value_products = jnp.where(
        causal_masking,
        jnp.einsum("ihe,jhe->hij", grad_heads, value_heads, preferred_element_type=jnp.float32),
        0.0,
    ).astype(jnp.bfloat16)
    query_products = jnp.where(
        causal_masking,
        jnp.einsum("ihd,jhd->hij", query_heads, key_heads, preferred_element_type=jnp.float32),
        0.0,
    ).astype(jnp.bfloat16)
    linear_branch_scale = (head_dim * row_count * seq_count) ** (-0.5)
    exact_precision = lax.Precision.HIGHEST
    linear_query = linear_branch_scale * (
        jnp.einsum(
            "ihe,hde->ihd",
            grad_heads.astype(jnp.float32),
            preceding_state,
            precision=exact_precision,
        )
        + jnp.einsum("hij,jhd->ihd", value_products, key_heads, preferred_element_type=jnp.float32)
    )
    lin_key = linear_branch_scale * (
        jnp.einsum(
            "jhe,hde->jhd",
            value_heads.astype(jnp.float32),
            gradient_following,
            precision=exact_precision,
        )
        + jnp.einsum(
            "hij,ihd->jhd", value_products, query_heads, preferred_element_type=jnp.float32
        )
    )
    linear_value = linear_branch_scale * (
        jnp.einsum(
            "jhd,hde->jhe",
            key_heads.astype(jnp.float32),
            gradient_following,
            precision=exact_precision,
        )
        + jnp.einsum("hij,ihe->jhe", query_products, grad_heads, preferred_element_type=jnp.float32)
    )
    window = WINDOW
    first_row = lax.axis_index("seq") * row_count
    halo_keys, halo_values = shifted(
        (key_heads[row_count - window :], value_heads[row_count - window :]), "seq", 1
    )
    keys_ext = jnp.concatenate([halo_keys, key_heads], axis=0)
    values_ext = jnp.concatenate([halo_values, value_heads], axis=0)
    win_query, key_ext_grad, value_ext_grad = window_block(
        query_heads, keys_ext, values_ext, grad_heads, first_row - window
    )
    carried_key, carried_value = (
        shifted(key_ext_grad[:window].astype(jnp.bfloat16), "seq", -1).astype(jnp.float32),
        shifted(value_ext_grad[:window].astype(jnp.bfloat16), "seq", -1).astype(jnp.float32),
    )
    padding = jnp.zeros((row_count - window, local_heads, head_dim), jnp.float32)
    win_key = key_ext_grad[window:] + jnp.concatenate([padding, carried_key], axis=0)
    win_value = value_ext_grad[window:] + jnp.concatenate([padding, carried_value], axis=0)
    query_grad = (linear_query + win_query).astype(jnp.bfloat16).reshape(row_count, features)
    key_grad = (lin_key + win_key).astype(jnp.bfloat16).reshape(row_count, features)
    value_grad = (linear_value + win_value).astype(jnp.bfloat16).reshape(row_count, features)
    return (resid_grad, query_grad, key_grad, value_grad)


def solution(mesh):
    return jax.shard_map(
        local,
        mesh=mesh,
        in_specs=(
            P(("groups", "seq"), ("sub", "rep")),
            P(("groups", "seq"), ("sub", "rep")),
            P(("groups", "seq"), None),
            P(("groups", "seq"), None),
            P("seq", ("sub", "rep"), None),
            P("seq", ("sub", "rep"), None),
            P("seq", None, ("sub", "rep")),
            P(("sub", "rep"), None),
            P(("groups", "seq"), ("sub", "rep")),
            P(("groups", "seq"), ("sub", "rep")),
            P(("groups", "seq"), ("sub", "rep")),
        ),
        out_specs=(
            P(("groups", "seq"), ("sub", "rep")),
            P(("groups", "seq"), ("sub", "rep")),
            P(("groups", "seq"), ("sub", "rep")),
            P(("groups", "seq"), ("sub", "rep")),
        ),
        check_vma=False,
    )
```

profile of v0, /device:TPU:0, one launch (start us, length us, event | category | flops | bytes accessed | tf_op | source)
XLA Modules:
  0.0 277.1 jit_solution(10073427366336069830)
XLA Ops:
  11.0 2.4 scatter_custom_fusion
  13.5 2.7 gather_fusion
  16.2 3.3 %gather_fusion.1 = bf16[768,512]{1,0:T(8,128)(2,1)} fusion(bf16[256,512]{1,0:T(8,128)(2,1)S(1)} %copy-done.2, s32[1024]{0:T(1024)S(1)} %pad_clamp_fusion.1), kind=kCustom, calls=%fused_computation.1 | custom fusion | bytes 1575936 | tf_op jit(solution)/shard_map/gather | solution.py:113
  19.6 2.2 broadcast_select_fusion
  21.8 26.3 %all_to_all.15 = bf16[4,2,96,512]{3,2,1,0:T(8,128)(2,1)} all-to-all(bf16[4,2,96,512]{3,2,1,0:T(8,128)(2,1)S(1)} %get-tuple-element.264), channel_id=1, replica_groups=mesh['groups'=2,'seq'=4,'sub'=2,'rep'=2] {'seq'}, dimensions={0} | all-to-all | bytes 1572864 | tf_op jit(solution)/shard_map/all_to_all | solution.py:119
  48.1 3.5 %all-to-all-start = ((bf16[4,2,96,512]{3,2,1,0:T(8,128)(2,1)}), bf16[4,2,96,512]{3,2,1,0:T(8,128)(2,1)S(1)}, u32[]{:S(2)}, u32[]{:S(2)}) async-start(bf16[4,2,96,512]{3,2,1,0:T(8,128)(2,1)} %get-tuple-element.265), calls=%async_computation | async-start | bytes 1572864 | tf_op jit(solution)/shard_map/all_to_all | solution.py:120
  51.7 3.6 %fusion.33 = bf16[4,2,96,768]{3,2,0,1:T(8,128)(2,1)} fusion(bf16[2,512,768]{2,1,0:T(8,128)(2,1)} %param.19, bf16[4,2,96,512]{3,2,1,0:T(8,128)(2,1)} %all_to_all.15), kind=kOutput, calls=%fused_computation.38 | convolution fusion | flops 604569600 | bytes 3538944 | tf_op jit(solution)/shard_map/nekf,efh->nekh/dot_general | solution.py:121
  55.3 1.8 fusion.39
  57.1 13.7 %all-to-all-done = bf16[4,2,96,512]{3,2,1,0:T(8,128)(2,1)S(1)} async-done(((bf16[4,2,96,512]{3,2,1,0:T(8,128)(2,1)}), bf16[4,2,96,512]{3,2,1,0:T(8,128)(2,1)S(1)}, u32[]{:S(2)}, u32[]{:S(2)}) %all-to-all-start) | async-done | bytes 786464 | tf_op jit(solution)/shard_map/all_to_all | solution.py:120
  70.8 3.3 %fusion.36 = bf16[4,2,96,768]{3,2,0,1:T(8,128)(2,1)} fusion(bf16[2,768,512]{2,1,0:T(8,128)(2,1)} %param.21, bf16[4,2,96,512]{3,2,1,0:T(8,128)(2,1)S(1)} %all-to-all-done), kind=kOutput, calls=%fused_computation.39 | convolution fusion | flops 604569600 | bytes 3538944 | tf_op jit(solution)/shard_map/nekf,ehf->nekh/dot_general | solution.py:123
  74.1 74.5 %all-reduce.5.cloned.1.call-done = (bf16[4,2,96,768]{3,2,0,1:T(8,128)(2,1)}, bf16[4,2,96,768]{3,2,0,1:T(8,128)(2,1)}, bf16[4,2,96,768]{3,2,0,1:T(8,128)(2,1)}) async-done(((bf16[4,2,96,768]{3,2,0,1:T(8,128)(2,1)}, bf16[4,2,96,768]{3,2,0,1:T(8,128)(2,1)}, bf16[4,2,96,768]{3,2,0,1:T(8,128)(2,1)}), (bf16[4,2,96,768]{3,2,0,1:T(8,128)(2,1)}, bf16[4,2,96,768]{3,2,0,1:T(8,128)(2,1)}, ...) | async-done | bytes 3538960 | tf_op jit(solution)/shard_map/psum | solution.py:128
  148.6 3.8 %fusion.11 = f32[2,4,96,512]{3,2,1,0:T(8,128)S(1)} fusion(bf16[2,512,768]{2,1,0:T(8,128)(2,1)} %param.19, bf16[4,2,96,768]{3,2,0,1:T(8,128)(2,1)} %get-tuple-element.261, bf16[4,2,96,768]{3,2,0,1:T(8,128)(2,1)} %get-tuple-element.262, bf16[4,2,96,768]{3,2,0,1:T(8,128)(2,1)} %get-tuple-element.263), kind=kOutput, calls=%fused_computation.21 | convolution fusion | flops 611647488 | bytes 6684672 | tf_op jit(solution)/shard_map/nekh,efh->nekf/dot_general | solution.py:130
  154.3 4.7 %all-to-all-start.2 = ((bf16[4,2,96,512]{3,2,1,0:T(8,128)(2,1)}), bf16[4,2,96,512]{3,2,1,0:T(8,128)(2,1)S(1)}, u32[]{:S(2)}, u32[]{:S(2)}) async-start(bf16[4,2,96,512]{3,2,1,0:T(8,128)(2,1)} %copy.90), calls=%async_computation.2 | async-start | bytes 1572864 | tf_op jit(solution)/shard_map/all_to_all | solution.py:135
  160.9 4.6 %collective-permute-start = (bf16[128,4,128]{2,0,1:T(8,128)(2,1)}, bf16[128,4,128]{2,0,1:T(8,128)(2,1)}, u32[]{:S(2)}, u32[]{:S(2)}) collective-permute-start(bf16[128,4,128]{2,0,1:T(8,128)(2,1)} %copy.99), channel_id=1, source_target_pairs={{0,4},{4,8},{8,12},{1,5},{5,9},{9,13},{2,6},{6,10},{10,14},{3,7},{... | collective-permute-start | bytes 393224 | tf_op jit(solution)/shard_map/ppermute | solution.py:27
  167.3 3.4 %collective-permute-start.1 = (bf16[128,4,128]{2,0,1:T(8,128)(2,1)}, bf16[128,4,128]{2,0,1:T(8,128)(2,1)}, u32[]{:S(2)}, u32[]{:S(2)}) collective-permute-start(bf16[128,4,128]{2,0,1:T(8,128)(2,1)} %copy.103), channel_id=1, source_target_pairs={{0,4},{4,8},{8,12},{1,5},{5,9},{9,13},{2,6},{6,10},{10,14},{3,7},{... | collective-permute-start | bytes 393224 | tf_op jit(solution)/shard_map/ppermute | solution.py:27
  172.1 25.1 %all-gather = bf16[16,128,128]{2,1,0:T(8,128)(2,1)} all-gather(bf16[4,128,128]{2,1,0:T(8,128)(2,1)S(1)} %convolution_convert_fusion.2), channel_id=2, replica_groups=mesh['groups'=2,'seq'=4,'sub'=2,'rep'=2] {'seq'}, dimensions={0}, use_global_device_ids=true | all-gather | bytes 655360 | tf_op jit(solution)/shard_map/all_gather | solution.py:12
  197.1 2.6 gather_fusion.2
  199.8 2.7 reshape.172
  202.4 2.6 multiply_reduce_fusion
  205.9 4.3 %while.30 = (s32[]{:T(128)}, f32[4,128,128]{2,1,0:T(8,128)S(1)}, s32[]{:T(128)}, bf16[4,4,128,128]{3,2,1,0:T(8,128)(2,1)}, s32[]{:T(128)}, /*index=5*/s32[]{:T(128)}) while((s32[]{:T(128)}, f32[4,128,128]{2,1,0:T(8,128)S(1)}, s32[]{:T(128)}, bf16[4,4,128,128]{3,2,1,0:T(8,128)(2,1)}, s32[]{:T(128)}, /*index=5*/s32[]{:T(128)}) %tuple.89), condition=%wide.region_9.10_spmd.clone, body=%wide.region_8.9_spmd.clone.sunk | while | flops 262148 | bytes 655453 | solution.py:21
  211.4 1.8 copy.170
  213.8 2.8 %fusion.110 = (f32[4,256]{1,0:T(4,128)S(1)}, f32[4,256,384]{1,2,0:T(8,128)}) fusion(pred[256,384]{0,1:T(8,128)(4,1)S(1)} %fusion.75, bf16[256,4,128]{2,0,1:T(8,128)(2,1)S(1)} %copy.100, bf16[128,4,128]{2,0,1:T(8,128)(2,1)} %collective-permute-done, bf16[256,512]{1,0:T(8,128)(2,1)} %param.23), kind=kOutput, calls=%fused_computation.138 | convolution fusion | flops 103022976 | bytes 2330624 | tf_op jit(solution)/shard_map/sub | solution.py:54
  216.6 3.7 %all-gather.4.cloned.1.call-done = bf16[256,2048]{1,0:T(8,128)(2,1)} async-done(((bf16[256,512]{1,0:T(8,128)(2,1)}), bf16[256,2048]{1,0:T(8,128)(2,1)}) %all-gather.4.cloned.1.call-update) | async-done | bytes 1048592 | tf_op jit(solution)/shard_map/all_gather | solution.py:144
  220.3 2.7 convolution_convert_fusion
  225.3 1.8 convolution_bitcast_fusion
  228.6 1.3 collective-permute-start.3
  230.6 19.5 %all-gather.1 = bf16[16,128,128]{2,1,0:T(8,128)(2,1)} all-gather(bf16[4,128,128]{2,1,0:T(8,128)(2,1)} %copy.114), channel_id=3, replica_groups=mesh['groups'=2,'seq'=4,'sub'=2,'rep'=2] {'seq'}, dimensions={0}, use_global_device_ids=true | all-gather | bytes 655360 | tf_op jit(solution)/shard_map/all_gather | solution.py:12
  250.1 4.3 %while.31 = (s32[]{:T(128)}, f32[4,128,128]{2,1,0:T(8,128)S(1)}, s32[]{:T(128)}, bf16[4,4,128,128]{3,2,1,0:T(8,128)(2,1)}, s32[]{:T(128)}, /*index=5*/s32[]{:T(128)}, s32[]{:T(128)}, s32[]{:T(128)}) while((s32[]{:T(128)}, f32[4,128,128]{2,1,0:T(8,128)S(1)}, s32[]{:T(128)}, bf16[4,4,128,128]{3,2,1,0:T(8,128)(2,1)}, s32[]{:T(128)}, ...), condition=%wide.region_14.15_spmd.clone, body=%wide.region_13.14_spmd.clone.sunk | while | flops 262152 | bytes 655515 | solution.py:21
  256.4 1.3 fusion.62
  260.1 1.3 collective-permute-start.2
  265.1 1.8 fusion.69
  267.7 1.6 fusion.71
  (109 shorter events, 36.0 us)
Async XLA Ops:
  7.2 213.1 %copy-start = (bf16[512,2048]{1,0:T(8,128)(2,1)S(1)}, bf16[512,2048]{1,0:T(8,128)(2,1)}, u32[]{:S(2)}) copy-start(bf16[512,2048]{1,0:T(8,128)(2,1)} %param.22) | copy-start | bytes 6291460
  7.2 6.3 %copy-start.1 = (bf16[256,512]{1,0:T(8,128)(2,1)S(1)}, bf16[256,512]{1,0:T(8,128)(2,1)}, u32[]{:S(2)}) copy-start(bf16[256,512]{1,0:T(8,128)(2,1)} %param.16) | copy-start | bytes 786436
  13.5 2.7 copy-start.2
  48.1 22.7 %all-to-all-start = ((bf16[4,2,96,512]{3,2,1,0:T(8,128)(2,1)}), bf16[4,2,96,512]{3,2,1,0:T(8,128)(2,1)S(1)}, u32[]{:S(2)}, u32[]{:S(2)}) async-start(bf16[4,2,96,512]{3,2,1,0:T(8,128)(2,1)} %get-tuple-element.265), calls=%async_computation | async-start | bytes 1572864 | tf_op jit(solution)/shard_map/all_to_all | solution.py:120
  51.6 97.0 %all-reduce.5.cloned.1.call-start = ((), (), s32[]{:S(2)}) async-start(), calls=%async_computation.4 | async-start | bytes 7077888 | tf_op jit(solution)/shard_map/psum | solution.py:128
  51.6 3.6 %copy-start.9 = (bf16[4,2,96,512]{3,2,1,0:T(8,128)(2,1)S(1)}, bf16[4,2,96,512]{3,2,1,0:T(8,128)(2,1)}, u32[]{:S(2)}) copy-start(bf16[4,2,96,512]{3,2,1,0:T(8,128)(2,1)} %all_to_all.15) | copy-start | bytes 2359300
  51.7 3.6 %copy-start.14 = (bf16[2,512,768]{2,1,0:T(8,128)(2,1)S(1)}, bf16[2,512,768]{2,1,0:T(8,128)(2,1)}, u32[]{:S(2)}) copy-start(bf16[2,512,768]{2,1,0:T(8,128)(2,1)} %param.20) | copy-start | bytes 4718596
  148.6 3.8 %copy-start.15 = (bf16[2,512,768]{2,1,0:T(8,128)(2,1)S(1)}, bf16[2,512,768]{2,1,0:T(8,128)(2,1)}, u32[]{:S(2)}) copy-start(bf16[2,512,768]{2,1,0:T(8,128)(2,1)} %param.20) | copy-start | bytes 4718596
  148.6 3.8 %copy-start.16 = (bf16[4,2,96,768]{3,2,0,1:T(8,128)(2,1)S(1)}, bf16[4,2,96,768]{3,2,0,1:T(8,128)(2,1)}, u32[]{:S(2)}) copy-start(bf16[4,2,96,768]{3,2,0,1:T(8,128)(2,1)} %get-tuple-element.261) | copy-start | bytes 3538948
  148.6 3.9 %copy-start.17 = (bf16[4,2,96,768]{3,2,0,1:T(8,128)(2,1)S(1)}, bf16[4,2,96,768]{3,2,0,1:T(8,128)(2,1)}, u32[]{:S(2)}) copy-start(bf16[4,2,96,768]{3,2,0,1:T(8,128)(2,1)} %get-tuple-element.262) | copy-start | bytes 3538948
  154.3 16.5 %copy-start.13 = (f32[256,2]{0,1:T(2,128)S(1)}, f32[256,2]{0,1:T(2,128)}, u32[]{:S(2)}) copy-start(f32[256,2]{0,1:T(2,128)} %param.18) | copy-start | bytes 6148
  154.3 42.9 %all-to-all-start.2 = ((bf16[4,2,96,512]{3,2,1,0:T(8,128)(2,1)}), bf16[4,2,96,512]{3,2,1,0:T(8,128)(2,1)S(1)}, u32[]{:S(2)}, u32[]{:S(2)}) async-start(bf16[4,2,96,512]{3,2,1,0:T(8,128)(2,1)} %copy.90), calls=%async_computation.2 | async-start | bytes 1572864 | tf_op jit(solution)/shard_map/all_to_all | solution.py:135
  159.0 61.3 %all-gather.4.cloned.1.call-start = ((), (), s32[]{:S(2)}) async-start(), calls=%async_computation.3 | async-start | bytes 1310720 | tf_op jit(solution)/shard_map/all_gather | solution.py:144
  160.1 0.8 copy-start.3
  160.9 52.9 %collective-permute-start = (bf16[128,4,128]{2,0,1:T(8,128)(2,1)}, bf16[128,4,128]{2,0,1:T(8,128)(2,1)}, u32[]{:S(2)}, u32[]{:S(2)}) collective-permute-start(bf16[128,4,128]{2,0,1:T(8,128)(2,1)} %copy.99), channel_id=1, source_target_pairs={{0,4},{4,8},{8,12},{1,5},{5,9},{9,13},{2,6},{6,10},{10,14},{3,7},{... | collective-permute-start | bytes 393224 | tf_op jit(solution)/shard_map/ppermute | solution.py:27
  167.3 89.1 %collective-permute-start.1 = (bf16[128,4,128]{2,0,1:T(8,128)(2,1)}, bf16[128,4,128]{2,0,1:T(8,128)(2,1)}, u32[]{:S(2)}, u32[]{:S(2)}) collective-permute-start(bf16[128,4,128]{2,0,1:T(8,128)(2,1)} %copy.103), channel_id=1, source_target_pairs={{0,4},{4,8},{8,12},{1,5},{5,9},{9,13},{2,6},{6,10},{10,14},{3,7},{... | collective-permute-start | bytes 393224 | tf_op jit(solution)/shard_map/ppermute | solution.py:27
  205.9 4.4 %copy-start.4 = (bf16[256,512]{0,1:T(8,128)(2,1)S(1)}, bf16[256,512]{0,1:T(8,128)(2,1)}, u32[]{:S(2)}) copy-start(bf16[256,512]{0,1:T(8,128)(2,1)} %copy-done.3) | copy-start | bytes 786436
  210.5 6.1 %copy-start.7 = (bf16[256,4,128]{2,0,1:T(8,128)(2,1)}, bf16[256,4,128]{2,0,1:T(8,128)(2,1)S(1)}, u32[]{:S(2)}) copy-start(bf16[256,4,128]{2,0,1:T(8,128)(2,1)S(1)} %copy.100) | copy-start | bytes 786436
  227.0 0.9 copy-start.12
  228.6 36.5 %collective-permute-start.3 = (bf16[128,4,128]{0,2,1:T(8,128)(2,1)}, bf16[128,4,128]{0,2,1:T(8,128)(2,1)}, u32[]{:S(2)}, u32[]{:S(2)}) collective-permute-start(bf16[128,4,128]{0,2,1:T(8,128)(2,1)} %slice.68), channel_id=1, source_target_pairs={{4,0},{8,4},{12,8},{5,1},{9,5},{13,9},{6,2},{10,6},{14,10},{7,3},{... | collective-permute-start | bytes 393224 | tf_op jit(solution)/shard_map/ppermute | solution.py:27
  250.1 4.3 %copy-start.10 = (pred[256,256]{1,0:T(8,128)(4,1)S(1)}, pred[256,256]{1,0:T(8,128)(4,1)}, u32[]{:S(2)}) copy-start(pred[256,256]{1,0:T(8,128)(4,1)} %iota_compare_fusion.2) | copy-start | bytes 196612
  254.4 1.0 copy-start.6
  254.8 1.6 copy-start.11
  254.8 1.6 copy-start.18
  259.0 2.8 %copy-start.8 = (bf16[256,4,128]{2,0,1:T(8,128)(2,1)S(1)}, bf16[256,4,128]{2,0,1:T(8,128)(2,1)}, u32[]{:S(2)}) copy-start(bf16[256,4,128]{2,0,1:T(8,128)(2,1)} %copy-done.7) | copy-start | bytes 786436
  259.3 3.7 %copy-start.5 = (f32[384,4,128]{0,2,1:T(8,128)}, f32[384,4,128]{0,2,1:T(8,128)S(1)}, u32[]{:S(2)}) copy-start(f32[384,4,128]{0,2,1:T(8,128)S(1)} %fusion.47) | copy-start | bytes 2359300
  260.1 7.6 %collective-permute-start.2 = (bf16[128,4,128]{0,2,1:T(8,128)(2,1)}, bf16[128,4,128]{0,2,1:T(8,128)(2,1)}, u32[]{:S(2)}, u32[]{:S(2)}) collective-permute-start(bf16[128,4,128]{0,2,1:T(8,128)(2,1)} %slice.69), channel_id=1, source_target_pairs={{4,0},{8,4},{12,8},{5,1},{9,5},{13,9},{6,2},{10,6},{14,10},{7,3},{... | collective-permute-start | bytes 393224 | tf_op jit(solution)/shard_map/ppermute | solution.py:27
Sparse Core Ops, SparseCore 0:
  74.2 74.3 all-reduce.4
  206.0 14.2 all-gather.3
where the time goes:
time: 278 us; the launch traced here: 277 us
  waiting for transfers between devices  92 us (33%)
  blocking collectives  70.9 us (26%)
  matrix products  33.8 us (12%)
  local copies, waits for them, and re-layouts  30.2 us (11%)
  starting transfers between devices  18.8 us (7%)
  other arithmetic  16.7 us (6%)
  between operations  14.5 us (5%)
    psum x1, waiting for transfers between devices, local(): lax.psum(hidden_part.astype(jnp.bfloat16), ('sub', 'rep'))  74.5 us
    all_gather x2, blocking collectives, entering(): everything = lax.all_gather(shard.astype(jnp.bfloat16), axis)  44.5 us
    all_to_all x1, blocking collectives, local(): lax.all_to_all(send_input, 'seq', split_axis=0, concat_axis=0, tiled=True)  26.3 us
    all_to_all x1, waiting for transfers between devices, local(): lax.all_to_all(send_grad, 'seq', split_axis=0, concat_axis=0, tiled=True)  13.7 us
    ppermute x4, starting transfers between devices, shifted(): return lax.ppermute(block, axis, route)  10.5 us
    select_n x8, other arithmetic, step(): return jnp.where(reached, new, before)  8.38 us
    unnamed x45, local copies, waits for them, and re-layouts  7.02 us
  transfers between devices with their start and end apart: 8, of which 3 were waited for; matrix products, arithmetic and copies ran while one was open for 19% of the time, Pallas kernels for 0%

commit v1 on v0

--- a/solution.py
+++ b/solution.py
@@ -1,10 +1,17 @@
+import functools
+
 import jax
 import jax.numpy as jnp
 from jax import lax
+from jax.experimental import pallas as pl
+from jax.experimental.pallas import tpu as pltpu
 from jax.sharding import PartitionSpec as P
 
 HEAD_DIM = 128
 WINDOW = 128
+MESH = pl.DeviceIdType.MESH
+F32 = jnp.float32
+BF16 = jnp.bfloat16
 
 
 def entering(shard, axis, combine, identity, reverse):
@@ -36,6 +43,388 @@
     gate_grad = hidden_grad * pre_up * sigmoid_gate * (1.0 + pre_gate * (1.0 - sigmoid_gate))
     up_grad = hidden_grad * pre_gate * sigmoid_gate
     return (gate_grad.astype(jnp.bfloat16), up_grad.astype(jnp.bfloat16))
+
+
+def dot(a, b):
+    return jnp.dot(a, b, preferred_element_type=F32)
+
+
+def dot_t(a, b):
+    return lax.dot_general(a, b, (((1,), (1,)), ((), ())), preferred_element_type=F32)
+
+
+def arrived(ref, sem):
+    pltpu.make_async_copy(ref, ref, sem).wait()
+
+
+def send(src, dst, send_sem, recv_sem, device):
+    copy = pltpu.make_async_remote_copy(
+        src_ref=src,
+        dst_ref=dst,
+        send_sem=send_sem,
+        recv_sem=recv_sem,
+        device_id=device,
+        device_id_type=MESH,
+    )
+    copy.start()
+    return copy
+
+
+def greet(axes):
+    barrier = pltpu.get_barrier_semaphore()
+    count = 0
+    for axis in axes:
+        size, me = lax.axis_size(axis), lax.axis_index(axis)
+        for off in range(1, size):
+            pl.semaphore_signal(
+                barrier, inc=1, device_id={axis: lax.rem(me + off, size)}, device_id_type=MESH
+            )
+            count += 1
+    pl.semaphore_wait(barrier, count)
+
+
+def slots_of(ids_t, cap, expert_count):
+    chosen, rows = ids_t.shape
+    experts = lax.broadcasted_iota(jnp.int32, (expert_count, rows), 0)
+    named = [(experts == ids_t[k : k + 1, :]).astype(F32) for k in range(chosen)]
+    earlier = (
+        lax.broadcasted_iota(jnp.int32, (rows, rows), 0)
+        < lax.broadcasted_iota(jnp.int32, (rows, rows), 1)
+    ).astype(BF16)
+    rank = dot(sum(named).astype(BF16), earlier)
+    first = experts.astype(F32) * cap + rank
+    return [jnp.sum(n * first, axis=0, keepdims=True) for n in named]
+
+
+def slots_of_rows(ids, cap, expert_count):
+    rows, chosen = ids.shape
+    experts = lax.broadcasted_iota(jnp.int32, (rows, expert_count), 1)
+    named = [(experts == ids[:, k : k + 1]).astype(F32) for k in range(chosen)]
+    earlier = (
+        lax.broadcasted_iota(jnp.int32, (rows, rows), 0)
+        > lax.broadcasted_iota(jnp.int32, (rows, rows), 1)
+    ).astype(BF16)
+    rank = dot(earlier, sum(named).astype(BF16))
+    first = experts.astype(F32) * cap + rank
+    return [jnp.sum(n * first, axis=1, keepdims=True) for n in named]
+
+
+def moe_kernel(
+    cap,
+    tile,
+    ids_ref,
+    ids_t_ref,
+    weight_ref,
+    input_ref,
+    upstream_ref,
+    gate_hbm,
+    up_hbm,
+    down_hbm,
+    resid_ref,
+    slots,
+    received,
+    w_gate,
+    w_up,
+    w_down,
+    part,
+    rep_in,
+    half,
+    sub_in,
+    grads,
+    out,
+    returned,
+    w_sem,
+    own_sem,
+    in_send,
+    in_recv,
+    rep_send,
+    rep_recv,
+    sub_send,
+    sub_recv,
+    agx_send,
+    agx_recv,
+    agr_send,
+    agr_recv,
+    out_send,
+    out_recv,
+):
+    seqs, subs, reps = lax.axis_size("seq"), lax.axis_size("sub"), lax.axis_size("rep")
+    seq, sub, rep = lax.axis_index("seq"), lax.axis_index("sub"), lax.axis_index("rep")
+    local_experts, features, hidden = gate_hbm.shape
+    experts = local_experts * seqs
+    half_rows = half.shape[2]
+    piece_rows = half_rows // subs
+    sent = []
+
+    weight_copies = [
+        pltpu.make_async_copy(gate_hbm, w_gate, w_sem.at[0]),
+        pltpu.make_async_copy(up_hbm, w_up, w_sem.at[1]),
+        pltpu.make_async_copy(down_hbm, w_down, w_sem.at[2]),
+    ]
+    for copy in weight_copies:
+        copy.start()
+
+    def slot_rows(owner, e):
+        return pl.ds(pl.multiple_of((owner * local_experts + e) * cap, 16), cap)
+
+    def source_rows(source):
+        return pl.ds(pl.multiple_of(source * cap, 16), cap)
+
+    def half_of(r):
+        return pl.ds(pl.multiple_of(r * half_rows, 16), half_rows)
+
+    def piece_of(s):
+        return pl.ds(pl.multiple_of(s * piece_rows, 16), piece_rows)
+
+    def rows_of(r, s):
+        return pl.ds(pl.multiple_of(r * half_rows + s * piece_rows, 16), piece_rows)
+
+    places = slots_of(ids_t_ref[...], cap, experts)
+    slot_count = experts * cap
+    slot_at = lax.broadcasted_iota(jnp.int32, (slot_count, places[0].shape[1]), 0).astype(F32)
+    pick = jnp.zeros(slot_at.shape, F32)
+    for place in places:
+        pick = pick + (slot_at == place).astype(F32)
+    pick = pick.astype(BF16)
+    slots[:, :features] = dot(pick, input_ref[...]).astype(BF16)
+    slots[:, features:] = dot(pick, upstream_ref[...]).astype(BF16)
+
+    greet(("seq", "sub", "rep"))
+
+    own = []
+    for e in range(local_experts):
+        copy = pltpu.make_async_copy(
+            slots.at[slot_rows(seq, e)], received.at[e, source_rows(seq)], own_sem.at[e]
+        )
+        copy.start()
+        own.append(copy)
+        batch = []
+        for off in range(1, seqs):
+            target = lax.rem(seq + off, seqs)
+            batch.append(
+                send(
+                    slots.at[slot_rows(target, e)],
+                    received.at[e, source_rows(seq)],
+                    in_send.at[e, off - 1],
+                    in_recv.at[e, off - 1],
+                    {"seq": target},
+                )
+            )
+        if e < local_experts - 1:
+            for copy in batch:
+                copy.wait_send()
+        else:
+            sent.extend(batch)
+    for copy in weight_copies:
+        copy.wait()
+
+    def first_products(e):
+        own[e].wait()
+        for off in range(1, seqs):
+            source = lax.rem(seq + seqs - off, seqs)
+            arrived(received.at[e, source_rows(source)], in_recv.at[e, off - 1])
+        for a in range(3):
+
+            @pl.loop(0, hidden // tile)
+            def _(j):
+                cols = pl.ds(pl.multiple_of(j * tile, tile), tile)
+                if a == 0:
+                    got = dot(received[e, :, :features], w_gate[e, :, cols])
+                elif a == 1:
+                    got = dot(received[e, :, :features], w_up[e, :, cols])
+                else:
+                    got = dot_t(received[e, :, features:], w_down[e, cols, :])
+                part[e, a, :, cols] = got.astype(BF16)
+
+            for off in range(1, reps):
+                target = lax.rem(rep + off, reps)
+                sent.append(
+                    send(
+                        part.at[e, a, half_of(target)],
+                        rep_in.at[e, a, off - 1],
+                        rep_send.at[e, a, off - 1],
+                        rep_recv.at[e, a, off - 1],
+                        {"rep": target},
+                    )
+                )
+        for a in range(3):
+            for off in range(1, reps):
+                arrived(rep_in.at[e, a, off - 1], rep_recv.at[e, a, off - 1])
+            total = part[e, a, half_of(rep), :].astype(F32)
+            for off in range(1, reps):
+                total = total + rep_in[e, a, off - 1].astype(F32)
+            half[e, a] = total.astype(BF16)
+            for off in range(1, subs):
+                target = lax.rem(sub + off, subs)
+                sent.append(
+                    send(
+                        half.at[e, a, piece_of(target)],
+                        sub_in.at[e, a, off - 1],
+                        sub_send.at[e, a, off - 1],
+                        sub_recv.at[e, a, off - 1],
+                        {"sub": target},
+                    )
+                )
+
+    def gate(e):
+        sums = []
+        for a in range(3):
+            for off in range(1, subs):
+                arrived(sub_in.at[e, a, off - 1], sub_recv.at[e, a, off - 1])
+            total = half[e, a, piece_of(sub), :].astype(F32)
+            for off in range(1, subs):
+                total = total + sub_in[e, a, off - 1].astype(F32)
+            sums.append(total)
+        gate_grad, up_grad = silu_grads(*sums)
+        mine = rows_of(rep, sub)
+        grads[e, mine, :hidden] = gate_grad
+        grads[e, mine, hidden:] = up_grad
+        for off in range(1, subs):
+            target = lax.rem(sub + off, subs)
+            sent.append(
+                send(
+                    grads.at[e, mine],
+                    grads.at[e, mine],
+                    agx_send.at[e, off - 1],
+                    agx_recv.at[e, off - 1],
+                    {"sub": target},
+                )
+            )
+        pass_on(e, 0)
+
+    def pass_on(e, sub_off):
+        piece = rows_of(rep, lax.rem(sub + subs - sub_off, subs))
+        for off in range(1, reps):
+            target = lax.rem(rep + off, reps)
+            sent.append(
+                send(
+                    grads.at[e, piece],
+                    grads.at[e, piece],
+                    agr_send.at[e, off - 1, sub_off],
+                    agr_recv.at[e, off - 1, sub_off],
+                    {"rep": target},
+                )
+            )
+
+    def second_products(e):
+        for sub_off in range(1, subs):
+            arrived(
+                grads.at[e, rows_of(rep, lax.rem(sub + subs - sub_off, subs))],
+                agx_recv.at[e, sub_off - 1],
+            )
+            pass_on(e, sub_off)
+        for off in range(1, reps):
+            for sub_off in range(subs):
+                piece = rows_of(
+                    lax.rem(rep + reps - off, reps), lax.rem(sub + subs - sub_off, subs)
+                )
+                arrived(grads.at[e, piece], agr_recv.at[e, off - 1, sub_off])
+
+        step = min(tile, features)
+
+        @pl.loop(0, features // step)
+        def _(j):
+            cols = pl.ds(pl.multiple_of(j * step, step), step)
+            got = dot_t(grads[e, :, :hidden], w_gate[e, cols, :])
+            got = got + dot_t(grads[e, :, hidden:], w_up[e, cols, :])
+            out[e, :, cols] = got.astype(BF16)
+
+        copy = pltpu.make_async_copy(
+            out.at[e, source_rows(seq)], returned.at[slot_rows(seq, e)], own_sem.at[e]
+        )
+        copy.start()
+        own[e] = copy
+        for off in range(1, seqs):
+            target = lax.rem(seq + off, seqs)
+            sent.append(
+                send(
+                    out.at[e, source_rows(target)],
+                    returned.at[slot_rows(seq, e)],
+                    out_send.at[e, off - 1],
+                    out_recv.at[e, off - 1],
+                    {"seq": target},
+                )
+            )
+
+    for e in range(local_experts):
+        first_products(e)
+        if e > 0:
+            second_products(e - 1)
+        gate(e)
+    second_products(local_experts - 1)
+
+    places = slots_of_rows(ids_ref[...], cap, experts)
+    rows = ids_ref.shape[0]
+    slot_at = lax.broadcasted_iota(jnp.int32, (rows, slot_count), 1).astype(F32)
+    for e in range(local_experts):
+        own[e].wait()
+        for off in range(1, seqs):
+            source = lax.rem(seq + seqs - off, seqs)
+            arrived(returned.at[slot_rows(source, e)], out_recv.at[e, off - 1])
+    combined = upstream_ref[...].astype(F32)
+    for k, place in enumerate(places):
+        pick = (slot_at == place).astype(BF16)
+        combined = combined + weight_ref[:, k : k + 1] * dot(pick, returned[...])
+    resid_ref[...] = combined.astype(BF16)
+    for copy in sent:
+        copy.wait_send()
+
+
+def moe_backward(moe_input, upstream, expert_ids, router_weight, w_gate, w_up, w_down):
+    rows, features = moe_input.shape
+    seqs, subs, reps = lax.axis_size("seq"), lax.axis_size("sub"), lax.axis_size("rep")
+    local_experts, _, hidden = w_gate.shape
+    experts = local_experts * seqs
+    cap = max(2, 3 * rows // experts)
+    cap = -(-cap // 16) * 16
+    while seqs * cap % (16 * subs * reps):
+        cap += 16
+    tile = 256 if hidden % 256 == 0 else hidden
+    block = seqs * cap
+    half_rows = block // reps
+    piece_rows = half_rows // subs
+    vmem = pl.BlockSpec(memory_space=pltpu.VMEM)
+    hbm = pl.BlockSpec(memory_space=pl.ANY)
+    dma = pltpu.SemaphoreType.DMA
+    n = local_experts
+    return pl.pallas_call(
+        functools.partial(moe_kernel, cap, tile),
+        out_shape=jax.ShapeDtypeStruct((rows, features), BF16),
+        in_specs=[vmem] * 5 + [hbm] * 3,
+        out_specs=vmem,
+        scratch_shapes=[
+            pltpu.VMEM((experts * cap, 2 * features), BF16),
+            pltpu.VMEM((n, block, 2 * features), BF16),
+            pltpu.VMEM(w_gate.shape, BF16),
+            pltpu.VMEM(w_up.shape, BF16),
+            pltpu.VMEM(w_down.shape, BF16),
+            pltpu.VMEM((n, 3, block, hidden), BF16),
+            pltpu.VMEM((n, 3, reps - 1, half_rows, hidden), BF16),
+            pltpu.VMEM((n, 3, half_rows, hidden), BF16),
+            pltpu.VMEM((n, 3, subs - 1, piece_rows, hidden), BF16),
+            pltpu.VMEM((n, block, 2 * hidden), BF16),
+            pltpu.VMEM((n, block, features), BF16),
+            pltpu.VMEM((experts * cap, features), BF16),
+            dma((3,)),
+            dma((n,)),
+            dma((n, seqs - 1)),
+            dma((n, seqs - 1)),
+            dma((n, 3, reps - 1)),
+            dma((n, 3, reps - 1)),
+            dma((n, 3, subs - 1)),
+            dma((n, 3, subs - 1)),
+            dma((n, subs - 1)),
+            dma((n, subs - 1)),
+            dma((n, reps - 1, subs)),
+            dma((n, reps - 1, subs)),
+            dma((n, seqs - 1)),
+            dma((n, seqs - 1)),
+        ],
+        compiler_params=pltpu.CompilerParams(
+            collective_id=0, has_side_effects=True, vmem_limit_bytes=56 * 1024 * 1024
+        ),
+        name="experts",
+    )(expert_ids, expert_ids.T, router_weight, moe_input, upstream, w_gate, w_up, w_down)
 
 
 def window_block(query_heads, keys_ext, values_ext, grad_heads, first_key):
@@ -91,55 +480,9 @@
 ):
     row_count, features = moe_input.shape
     seq_count = lax.axis_size("seq")
-    local_experts = w_gate.shape[0]
-    expert_count = local_experts * seq_count
-    capacity = max(2, 3 * row_count // expert_count)
-    chosen = expert_ids.shape[1]
-    pair_ids = expert_ids.reshape(-1)
-    pair_count = pair_ids.shape[0]
-    one_hot = (pair_ids[:, None] == jnp.arange(expert_count, dtype=jnp.int32)[None, :]).astype(
-        jnp.int32
-    )
-    slot_rank = jnp.sum((jnp.cumsum(one_hot, axis=0) - one_hot) * one_hot, axis=1)
-    slot_index = pair_ids * capacity + slot_rank
-    slot_owner = (
-        jnp.zeros((expert_count * capacity,), jnp.int32)
-        .at[slot_index]
-        .set(jnp.arange(pair_count, dtype=jnp.int32) + 1)
-    )
-    live_slot = (slot_owner > 0)[:, None]
-    token_row = jnp.maximum(slot_owner - 1, 0) // chosen
-    slot_shape = (seq_count, local_experts, capacity, features)
-    send_input = jnp.where(live_slot, moe_input[token_row], jnp.zeros((), jnp.bfloat16)).reshape(
-        slot_shape
-    )
-    send_grad = jnp.where(live_slot, upstream[token_row], jnp.zeros((), jnp.bfloat16)).reshape(
-        slot_shape
-    )
-    slot_input = lax.all_to_all(send_input, "seq", split_axis=0, concat_axis=0, tiled=True)
-    slot_grad = lax.all_to_all(send_grad, "seq", split_axis=0, concat_axis=0, tiled=True)
-    gate_part = jnp.einsum("nekf,efh->nekh", slot_input, w_gate, preferred_element_type=jnp.float32)
-    up_part = jnp.einsum("nekf,efh->nekh", slot_input, w_up, preferred_element_type=jnp.float32)
-    hidden_part = jnp.einsum(
-        "nekf,ehf->nekh", slot_grad, w_down, preferred_element_type=jnp.float32
-    )
-    pre_gate = lax.psum(gate_part.astype(jnp.bfloat16), ("sub", "rep")).astype(jnp.float32)
-    pre_up = lax.psum(up_part.astype(jnp.bfloat16), ("sub", "rep")).astype(jnp.float32)
-    hidden_grad = lax.psum(hidden_part.astype(jnp.bfloat16), ("sub", "rep")).astype(jnp.float32)
-    gate_grad, up_grad = silu_grads(pre_gate, pre_up, hidden_grad)
-    input_grad = jnp.einsum("nekh,efh->nekf", gate_grad, w_gate, preferred_element_type=jnp.float32)
-    input_grad = input_grad + jnp.einsum(
-        "nekh,efh->nekf", up_grad, w_up, preferred_element_type=jnp.float32
-    )
-    expert_out = input_grad.astype(jnp.bfloat16)
-    returned = lax.all_to_all(expert_out, "seq", split_axis=0, concat_axis=0, tiled=True).reshape(
-        expert_count * capacity, features
-    )
-    pair_grads = returned[slot_index].astype(jnp.float32) * router_weight.reshape(-1)[:, None]
-    combined = upstream.astype(jnp.float32) + jnp.sum(
-        pair_grads.reshape(row_count, chosen, features), axis=1
-    )
-    resid_grad = combined.astype(jnp.bfloat16)
+    resid_grad = moe_backward(
+        moe_input, upstream, expert_ids, router_weight, w_gate, w_up, w_down
+    )
     head_grad = lax.dot_general(
         lax.all_gather(resid_grad, ("sub", "rep"), axis=1, tiled=True),
         out_proj,

time: 278 us -> 179 us (0.64)
  waiting for transfers between devices: 92 us -> 2.5 us
  Pallas kernels: 0 us -> 80.8 us
  blocking collectives: 70.9 us -> 33.8 us
  matrix products: 33.8 us -> 18.7 us
  local copies, waits for them, and re-layouts: 30.2 us -> 15.3 us
  other arithmetic: 16.7 us -> 5.4 us
  starting transfers between devices: 18.8 us -> 7.61 us
    pallas_call x0 -> x1, Pallas kernels: none -> 80.8 us  [moe_backward(): pl.pallas_call(functools.partial(moe_kernel, cap, tile), out_shape=jax.Sh...]
    psum x1 -> x0, waiting for transfers between devices: 74.5 us -> none  [local(): lax.psum(hidden_part.astype(jnp.bfloat16), ('sub', 'rep'))]
    all_to_all x1 -> x0, blocking collectives: 26.3 us -> none  [local(): lax.all_to_all(send_input, 'seq', split_axis=0, concat_axis=0, tiled=True)]
    all_to_all x2 -> x0, waiting for transfers between devices: 13.7 us -> none  [the longest x1 13.7 us: local(): lax.all_to_all(send_grad, 'seq', split_axis=0, concat_axis=0, tiled=True)]
    dot_general x5 -> x0, matrix products: 13.4 us -> none  [the longest x1 3.83 us: local(): jnp.einsum('nekh,efh->nekf', gate_grad, w_gate, preferred_element_type=jn...]
    all_gather x2, blocking collectives: 44.5 us -> 33.8 us  [entering(): everything = lax.all_gather(shard.astype(jnp.bfloat16), axis)]
    gather x3 -> x0, local copies, waits for them, and re-layouts: 8.64 us -> none  [the longest x1 3.31 us: local(): moe_input[token_row]]
    all_to_all x2 -> x0, starting transfers between devices: 8.22 us -> none  [the longest x1 4.73 us: local(): lax.all_to_all(expert_out, 'seq', split_axis=0, concat_axis=0, tiled=True)]
  transfers between devices with their start and end apart: 8 -> 5, of which waited for: 3 -> 1; matrix products, arithmetic and copies ran while one was open for 19% -> 14% of each run, Pallas kernels for 0% -> 0%
where the time goes in v1:
time: 179 us
  Pallas kernels  80.8 us (45%)
  blocking collectives  33.8 us (19%)
  matrix products  18.7 us (10%)
  local copies, waits for them, and re-layouts  15.3 us (9%)
  between operations  14.3 us (8%)
  starting transfers between devices  7.61 us (4%)
  other arithmetic  5.4 us (3%)
  waiting for transfers between devices  2.5 us (1%)
    pallas_call x1, Pallas kernels, moe_backward(): pl.pallas_call(functools.partial(moe_kernel, cap, tile), out_shape=jax.Sh...  80.8 us
    all_gather x2, blocking collectives, entering(): everything = lax.all_gather(shard.astype(jnp.bfloat16), axis)  33.8 us
    ppermute x4, starting transfers between devices, shifted(): return lax.ppermute(block, axis, route)  7.57 us
    unnamed x36, local copies, waits for them, and re-layouts  6.91 us
    select_n x8, other arithmetic, step(): return jnp.where(reached, new, before)  4.6 us
  transfers between devices with their start and end apart: 5, of which 1 were waited for; matrix products, arithmetic and copies ran while one was open for 14% of the time, Pallas kernels for 0%

profile of v1, /device:TPU:0, one launch (start us, length us, event | category | flops | bytes accessed | tf_op | source)
XLA Modules:
  0.0 178.6 jit_solution(7256707488935588916)
XLA Ops:
  7.2 1.6 copy.79.ids_ref
  8.8 1.5 copy.80.weight_ref
  10.3 80.8 %experts.1 = bf16[256,512]{1,0:T(8,128)(2,1)} custom-call(s32[256,2]{1,0:T(8,128)} %copy.79.ids_ref, s32[2,256]{1,0:T(2,128)} %bitcast.148, f32[256,2]{1,0:T(8,128)} %copy.80.weight_ref, bf16[256,512]{1,0:T(8,128)(2,1)} %input_ref.1, bf16[256,512]{1,0:T(8,128)(2,1)} %upstream_ref.1, bf16[2,512,768]{2,1,0:T(8,128)(2,1)} %gate_hbm.1, ...), custom_call_target="tpu_custom_call" | custom-call | tf_op jit(solution)/shard_map/experts/pallas_call | solution.py:390
  92.1 3.1 %collective-permute-start.1 = (bf16[128,4,128]{2,0,1:T(8,128)(2,1)}, bf16[128,4,128]{2,0,1:T(8,128)(2,1)}, u32[]{:S(2)}, u32[]{:S(2)}) collective-permute-start(bf16[128,4,128]{2,0,1:T(8,128)(2,1)} %copy.92), channel_id=1, source_target_pairs={{0,4},{4,8},{8,12},{1,5},{5,9},{9,13},{2,6},{6,10},{10,14},{3,7},{... | collective-permute-start | bytes 393224 | tf_op jit(solution)/shard_map/ppermute | solution.py:34
  96.1 1.9 %collective-permute-start = (bf16[128,4,128]{2,0,1:T(8,128)(2,1)}, bf16[128,4,128]{2,0,1:T(8,128)(2,1)}, u32[]{:S(2)}, u32[]{:S(2)}) collective-permute-start(bf16[128,4,128]{2,0,1:T(8,128)(2,1)} %copy.88), channel_id=1, source_target_pairs={{0,4},{4,8},{8,12},{1,5},{5,9},{9,13},{2,6},{6,10},{10,14},{3,7},{... | collective-permute-start | bytes 393224 | tf_op jit(solution)/shard_map/ppermute | solution.py:34
  98.2 16.7 %all-gather = bf16[16,128,128]{2,1,0:T(8,128)(2,1)S(1)} all-gather(bf16[4,128,128]{2,1,0:T(8,128)(2,1)S(1)} %convolution_convert_fusion.2), channel_id=2, replica_groups=mesh['groups'=2,'seq'=4,'sub'=2,'rep'=2] {'seq'}, dimensions={0}, use_global_device_ids=true | all-gather | bytes 655360 | tf_op jit(solution)/shard_map/all_gather | solution.py:19
  117.3 1.9 %copy.150 = bf16[256,512]{0,1:T(8,128)(2,1)} copy(bf16[256,512]{1,0:T(8,128)(2,1)} %param.23) | data formatting | bytes 524288 | tf_op jit(solution)/shard_map/reshape | solution.py:495
  119.3 2.9 %fusion.55 = (f32[4,256]{1,0:T(4,128)S(1)}, f32[4,256,384]{1,2,0:T(8,128)}) fusion(pred[256,384]{0,1:T(8,128)(4,1)} %fusion.28, bf16[256,4,128]{2,0,1:T(8,128)(2,1)S(1)} %copy.89, bf16[128,4,128]{2,0,1:T(8,128)(2,1)} %collective-permute-done, bf16[256,512]{1,0:T(8,128)(2,1)} %param.23), kind=kOutput, calls=%fused_computation.73 | convolution fusion | flops 103022976 | bytes 2330624 | tf_op jit(solution)/shard_map/sub | solution.py:443
  122.1 2.7 %convolution_convert_fusion = bf16[256,512]{1,0:T(8,128)(2,1)} fusion(bf16[256,2048]{1,0:T(8,128)(2,1)} %all-gather.4.cloned.1.call-done, bf16[512,2048]{1,0:T(8,128)(2,1)S(1)} %copy-done), kind=kOutput, calls=%fused_computation.32 | convolution fusion | flops 537001984 | bytes 3407872 | tf_op jit(solution)/shard_map/dot_general | solution.py:486
  124.8 1.1 copy.131
  126.9 1.0 convolution_bitcast_fusion.1
  127.9 1.3 convolution_bitcast_fusion
  129.4 1.3 fusion.18
  130.7 1.3 multiply_convert_fusion
  132.0 1.3 fusion.5
  133.6 1.3 fusion.17
  134.9 0.8 copy.115
  135.8 1.0 slice.53
  136.7 1.3 collective-permute-start.2
  138.2 17.1 %all-gather.1 = bf16[16,128,128]{2,1,0:T(8,128)(2,1)} all-gather(bf16[4,128,128]{2,1,0:T(8,128)(2,1)S(1)} %copy.103), channel_id=3, replica_groups=mesh['groups'=2,'seq'=4,'sub'=2,'rep'=2] {'seq'}, dimensions={0}, use_global_device_ids=true | all-gather | bytes 655360 | tf_op jit(solution)/shard_map/all_gather | solution.py:19
  155.2 4.2 %while.31 = (s32[]{:T(128)}, f32[4,128,128]{2,1,0:T(8,128)S(1)}, s32[]{:T(128)}, bf16[4,4,128,128]{3,2,1,0:T(8,128)(2,1)}, s32[]{:T(128)}, /*index=5*/s32[]{:T(128)}, s32[]{:T(128)}, s32[]{:T(128)}) while((s32[]{:T(128)}, f32[4,128,128]{2,1,0:T(8,128)S(1)}, s32[]{:T(128)}, bf16[4,4,128,128]{3,2,1,0:T(8,128)(2,1)}, s32[]{:T(128)}, ...), condition=%wide.region_6.7_spmd.clone, body=%wide.region_5.6_spmd.clone.sunk | while | flops 262152 | bytes 655523 | solution.py:28
  155.2 1.0 add_select_fusion.5
  156.3 1.0 add_select_fusion.5
  157.3 1.0 add_select_fusion.5
  158.4 1.0 add_select_fusion.5
  159.5 1.7 slice.52
  161.2 1.3 collective-permute-start.3
  162.5 1.2 fusion.58
  163.7 1.3 fusion.24
  165.1 0.8 copy.116
  165.9 2.5 %collective-permute-done.3 = bf16[128,4,128]{0,2,1:T(8,128)(2,1)} collective-permute-done((bf16[128,4,128]{0,2,1:T(8,128)(2,1)}, bf16[128,4,128]{0,2,1:T(8,128)(2,1)}, u32[]{:S(2)}, u32[]{:S(2)}) %collective-permute-start.3) | collective-permute-done | bytes 131104 | tf_op jit(solution)/shard_map/ppermute | solution.py:34
  168.4 1.8 fusion.22
  (61 shorter events, 8.1 us)
Async XLA Ops:
  7.2 115.0 %copy-start = (bf16[512,2048]{1,0:T(8,128)(2,1)S(1)}, bf16[512,2048]{1,0:T(8,128)(2,1)}, u32[]{:S(2)}) copy-start(bf16[512,2048]{1,0:T(8,128)(2,1)} %param.22) | copy-start | bytes 6291460
  7.2 115.0 %all-gather.4.cloned.1.call-start = ((), (), s32[]{:S(2)}) async-start(), calls=%async_computation | async-start | bytes 1310720 | tf_op jit(solution)/shard_map/all_gather | solution.py:487
  10.3 80.8 %copy-start.10 = (bf16[256,512]{1,0:T(8,128)(2,1)S(1)}, bf16[256,512]{1,0:T(8,128)(2,1)}, u32[]{:S(2)}) copy-start(bf16[256,512]{1,0:T(8,128)(2,1)} %param.25) | copy-start | bytes 786436
  10.3 84.8 %copy-start.11 = (bf16[256,512]{1,0:T(8,128)(2,1)S(1)}, bf16[256,512]{1,0:T(8,128)(2,1)}, u32[]{:S(2)}) copy-start(bf16[256,512]{1,0:T(8,128)(2,1)} %param.24) | copy-start | bytes 786436
  92.1 37.3 %collective-permute-start.1 = (bf16[128,4,128]{2,0,1:T(8,128)(2,1)}, bf16[128,4,128]{2,0,1:T(8,128)(2,1)}, u32[]{:S(2)}, u32[]{:S(2)}) collective-permute-start(bf16[128,4,128]{2,0,1:T(8,128)(2,1)} %copy.92), channel_id=1, source_target_pairs={{0,4},{4,8},{8,12},{1,5},{5,9},{9,13},{2,6},{6,10},{10,14},{3,7},{... | collective-permute-start | bytes 393224 | tf_op jit(solution)/shard_map/ppermute | solution.py:34
  96.1 23.2 %collective-permute-start = (bf16[128,4,128]{2,0,1:T(8,128)(2,1)}, bf16[128,4,128]{2,0,1:T(8,128)(2,1)}, u32[]{:S(2)}, u32[]{:S(2)}) collective-permute-start(bf16[128,4,128]{2,0,1:T(8,128)(2,1)} %copy.88), channel_id=1, source_target_pairs={{0,4},{4,8},{8,12},{1,5},{5,9},{9,13},{2,6},{6,10},{10,14},{3,7},{... | collective-permute-start | bytes 393224 | tf_op jit(solution)/shard_map/ppermute | solution.py:34
  117.3 4.8 %copy-start.5 = (bf16[256,4,128]{2,0,1:T(8,128)(2,1)}, bf16[256,4,128]{2,0,1:T(8,128)(2,1)S(1)}, u32[]{:S(2)}) copy-start(bf16[256,4,128]{2,0,1:T(8,128)(2,1)S(1)} %copy.89) | copy-start | bytes 786436
  119.3 6.7 %copy-start.8 = (pred[256,256]{1,0:T(8,128)(4,1)}, pred[256,256]{1,0:T(8,128)(4,1)S(1)}, u32[]{:S(2)}) copy-start(pred[256,256]{1,0:T(8,128)(4,1)S(1)} %iota_compare_fusion.2) | copy-start | bytes 196612
  125.9 1.0 copy-start.2
  126.3 1.6 copy-start.13
  127.9 1.3 copy-start.7
  127.9 1.5 copy-start.12
  132.0 1.7 copy-start.6
  136.7 27.0 %collective-permute-start.2 = (bf16[128,4,128]{0,2,1:T(8,128)(2,1)S(1)}, bf16[128,4,128]{0,2,1:T(8,128)(2,1)}, u32[]{:S(2)}, u32[]{:S(2)}) collective-permute-start(bf16[128,4,128]{0,2,1:T(8,128)(2,1)S(1)} %slice.53), channel_id=1, source_target_pairs={{4,0},{8,4},{12,8},{5,1},{9,5},{13,9},{6,2},{10,6},{14,10},{7,3},{... | collective-permute-start | bytes 393224 | tf_op jit(solution)/shard_map/ppermute | solution.py:34
  159.5 4.3 %copy-start.1 = (f32[384,4,128]{0,2,1:T(8,128)S(1)}, f32[384,4,128]{0,2,1:T(8,128)}, u32[]{:S(2)}) copy-start(f32[384,4,128]{0,2,1:T(8,128)} %fusion.5) | copy-start | bytes 2359300
  159.5 4.3 %copy-start.4 = (f32[256,4,128]{0,2,1:T(8,128)S(1)}, f32[256,4,128]{0,2,1:T(8,128)}, u32[]{:S(2)}) copy-start(f32[256,4,128]{0,2,1:T(8,128)} %convolution_bitcast_fusion.1) | copy-start | bytes 1572868
  161.2 7.2 %collective-permute-start.3 = (bf16[128,4,128]{0,2,1:T(8,128)(2,1)}, bf16[128,4,128]{0,2,1:T(8,128)(2,1)}, u32[]{:S(2)}, u32[]{:S(2)}) collective-permute-start(bf16[128,4,128]{0,2,1:T(8,128)(2,1)} %slice.52), channel_id=1, source_target_pairs={{4,0},{8,4},{12,8},{5,1},{9,5},{13,9},{6,2},{10,6},{14,10},{7,3},{... | collective-permute-start | bytes 393224 | tf_op jit(solution)/shard_map/ppermute | solution.py:34
  162.5 5.9 %copy-start.9 = (pred[256,256]{1,0:T(8,128)(4,1)S(1)}, pred[256,256]{1,0:T(8,128)(4,1)}, u32[]{:S(2)}) copy-start(pred[256,256]{1,0:T(8,128)(4,1)} %copy-done.8) | copy-start | bytes 196612
  165.9 5.1 %copy-start.3 = (bf16[256,512]{1,0:T(8,128)(2,1)S(1)}, bf16[256,512]{1,0:T(8,128)(2,1)}, u32[]{:S(2)}) copy-start(bf16[256,512]{1,0:T(8,128)(2,1)} %experts.1) | copy-start | bytes 786436
Sparse Core Ops, SparseCore 0:
  91.3 16.2 all-gather.3

commit v2 on v1

--- a/solution.py
+++ b/solution.py
@@ -12,30 +12,6 @@
 MESH = pl.DeviceIdType.MESH
 F32 = jnp.float32
 BF16 = jnp.bfloat16
-
-
-def entering(shard, axis, combine, identity, reverse):
-    length, index = (lax.axis_size(axis), lax.axis_index(axis))
-    everything = lax.all_gather(shard.astype(jnp.bfloat16), axis)
-    start = jnp.broadcast_to(jnp.asarray(identity, shard.dtype), shard.shape)
-
-    def step(k, before):
-        at = length - 1 - k if reverse else k
-        reached = at > index if reverse else at < index
-        new = combine(before, everything[at].astype(shard.dtype))
-        return jnp.where(reached, new, before)
-
-    return lax.fori_loop(0, length, step, start)
-
-
-def shifted(block, axis, distance):
-    devices = range(lax.axis_size(axis))
-    route = [(i - distance, i) for i in devices if i - distance in devices]
-    return lax.ppermute(block, axis, route)
-
-
-def add_single(before_part, after_part):
-    return before_part + after_part
 
 
 def silu_grads(pre_gate, pre_up, hidden_grad):
@@ -96,31 +72,36 @@
     return [jnp.sum(n * first, axis=0, keepdims=True) for n in named]
 
 
-def slots_of_rows(ids, cap, expert_count):
-    rows, chosen = ids.shape
-    experts = lax.broadcasted_iota(jnp.int32, (rows, expert_count), 1)
-    named = [(experts == ids[:, k : k + 1]).astype(F32) for k in range(chosen)]
-    earlier = (
-        lax.broadcasted_iota(jnp.int32, (rows, rows), 0)
-        > lax.broadcasted_iota(jnp.int32, (rows, rows), 1)
-    ).astype(BF16)
-    rank = dot(earlier, sum(named).astype(BF16))
-    first = experts.astype(F32) * cap + rank
-    return [jnp.sum(n * first, axis=1, keepdims=True) for n in named]
-
-
-def moe_kernel(
+def as_column(line):
+    count = line.shape[1]
+    same = lax.broadcasted_iota(jnp.int32, (count, count), 0) == lax.broadcasted_iota(
+        jnp.int32, (count, count), 1
+    )
+    return jnp.sum(jnp.where(same, line, 0.0), axis=1, keepdims=True)
+
+
+def dot_0(a, b):
+    return lax.dot_general(a, b, (((0,), (0,)), ((), ())), preferred_element_type=F32)
+
+
+def kernel(
     cap,
     tile,
     ids_ref,
-    ids_t_ref,
     weight_ref,
     input_ref,
     upstream_ref,
+    query_ref,
+    key_ref,
+    value_ref,
     gate_hbm,
     up_hbm,
     down_hbm,
+    proj_hbm,
     resid_ref,
+    query_grad_ref,
+    key_grad_ref,
+    value_grad_ref,
     slots,
     received,
     w_gate,
@@ -133,6 +114,25 @@
     grads,
     out,
     returned,
+    proj,
+    keys_ext,
+    values_ext,
+    probs,
+    attended,
+    query_dots,
+    state,
+    state_in,
+    before,
+    grad_state,
+    grad_state_in,
+    after,
+    full,
+    head_grad,
+    query_sum,
+    key_sum,
+    value_sum,
+    carry,
+    carry_in,
     w_sem,
     own_sem,
     in_send,
@@ -147,6 +147,18 @@
     agr_recv,
     out_send,
     out_recv,
+    halo_send,
+    halo_recv,
+    state_send,
+    state_recv,
+    after_send,
+    after_recv,
+    resx_send,
+    resx_recv,
+    resr_send,
+    resr_recv,
+    carry_send,
+    carry_recv,
 ):
     seqs, subs, reps = lax.axis_size("seq"), lax.axis_size("sub"), lax.axis_size("rep")
     seq, sub, rep = lax.axis_index("seq"), lax.axis_index("sub"), lax.axis_index("rep")
@@ -155,11 +167,32 @@
     half_rows = half.shape[2]
     piece_rows = half_rows // subs
     sent = []
+    sent_if = []
+    rows = ids_ref.shape[1]
+    heads = features // HEAD_DIM
+    window = WINDOW
+    pieces = subs * reps
+
+    def send_if(cond, src, dst, send_sem, recv_sem, device):
+        copy = pltpu.make_async_remote_copy(
+            src_ref=src,
+            dst_ref=dst,
+            send_sem=send_sem,
+            recv_sem=recv_sem,
+            device_id=device,
+            device_id_type=MESH,
+        )
+        pl.when(cond)(copy.start)
+        sent_if.append((cond, copy))
+
+    def of_head(h):
+        return pl.ds(h * HEAD_DIM, HEAD_DIM)
 
     weight_copies = [
         pltpu.make_async_copy(gate_hbm, w_gate, w_sem.at[0]),
         pltpu.make_async_copy(up_hbm, w_up, w_sem.at[1]),
         pltpu.make_async_copy(down_hbm, w_down, w_sem.at[2]),
+        pltpu.make_async_copy(proj_hbm, proj, w_sem.at[3]),
     ]
     for copy in weight_copies:
         copy.start()
@@ -179,7 +212,7 @@
     def rows_of(r, s):
         return pl.ds(pl.multiple_of(r * half_rows + s * piece_rows, 16), piece_rows)
 
-    places = slots_of(ids_t_ref[...], cap, experts)
+    places = slots_of(ids_ref[...], cap, experts)
     slot_count = experts * cap
     slot_at = lax.broadcasted_iota(jnp.int32, (slot_count, places[0].shape[1]), 0).astype(F32)
     pick = jnp.zeros(slot_at.shape, F32)
@@ -346,31 +379,250 @@
                 )
             )
 
+    def own_parts():
+        keys_ext[window:, :] = key_ref[...]
+        values_ext[window:, :] = value_ref[...]
+
+        @pl.when(seq == 0)
+        def _():
+            keys_ext[:window, :] = jnp.zeros((window, features), BF16)
+            values_ext[:window, :] = jnp.zeros((window, features), BF16)
+
+        @pl.when(seq == seqs - 1)
+        def _():
+            carry_in[...] = jnp.zeros(carry_in.shape, BF16)
+
+        causal = lax.broadcasted_iota(jnp.int32, (rows, rows), 0) >= lax.broadcasted_iota(
+            jnp.int32, (rows, rows), 1
+        )
+        for h in range(heads):
+            cols = of_head(h)
+            q, k, v = query_ref[:, cols], key_ref[:, cols], value_ref[:, cols]
+            state[h] = dot_0(k, v).astype(BF16)
+            query_dots[h] = jnp.where(causal, dot_t(q, k), 0.0).astype(BF16)
+        before[...] = jnp.zeros(before.shape, F32)
+        after[...] = jnp.zeros(after.shape, F32)
+
+    def send_own_parts():
+        tail = pl.ds(rows - window, window)
+        for n, (src, dst) in enumerate(((key_ref, keys_ext), (value_ref, values_ext))):
+            send_if(
+                seq < seqs - 1,
+                src.at[tail],
+                dst.at[pl.ds(0, window)],
+                halo_send.at[n],
+                halo_recv.at[n],
+                {"seq": lax.rem(seq + 1, seqs)},
+            )
+        for off in range(1, seqs):
+            send_if(
+                seq + off < seqs,
+                state,
+                state_in.at[off - 1],
+                state_send.at[off - 1],
+                state_recv.at[off - 1],
+                {"seq": lax.rem(seq + off, seqs)},
+            )
+
+    def window_probs():
+        @pl.when(seq > 0)
+        def _():
+            for n, dst in enumerate((keys_ext, values_ext)):
+                arrived(dst.at[pl.ds(0, window)], halo_recv.at[n])
+
+        shape = (rows, rows + window)
+        query_pos = lax.broadcasted_iota(jnp.int32, shape, 0)
+        key_pos = lax.broadcasted_iota(jnp.int32, shape, 1)
+        allowed = (
+            (key_pos > query_pos)
+            & (key_pos <= query_pos + window)
+            & (key_pos + (seq * rows - window) >= 0)
+        )
+        for h in range(heads):
+            cols = of_head(h)
+            scores = dot_t(query_ref[:, cols], keys_ext[:, cols]) * (HEAD_DIM**-0.5)
+            scores = jnp.where(allowed, scores, -jnp.inf)
+            weights = jnp.exp(scores - jnp.max(scores, axis=1, keepdims=True))
+            softmax = weights / jnp.sum(weights, axis=1, keepdims=True)
+            probs[h] = softmax
+            attended[:, cols] = dot(softmax.astype(BF16), values_ext[:, cols])
+
+    def states_before():
+        for off in range(1, seqs):
+
+            @pl.when(seq >= off)
+            def _():
+                arrived(state_in.at[off - 1], state_recv.at[off - 1])
+                before[...] = before[...] + state_in[off - 1].astype(F32)
+
+    own_parts()
     for e in range(local_experts):
         first_products(e)
+        if e == local_experts - 1:
+            send_own_parts()
         if e > 0:
             second_products(e - 1)
+        if e == local_experts - 1:
+            window_probs()
+            states_before()
         gate(e)
     second_products(local_experts - 1)
 
-    places = slots_of_rows(ids_ref[...], cap, experts)
-    rows = ids_ref.shape[0]
+    columns = [as_column(place) for place in places]
+    pair_weights = [as_column(weight_ref[k : k + 1, :]) for k in range(len(places))]
     slot_at = lax.broadcasted_iota(jnp.int32, (rows, slot_count), 1).astype(F32)
+    picks = [(slot_at == column).astype(BF16) for column in columns]
     for e in range(local_experts):
         own[e].wait()
         for off in range(1, seqs):
             source = lax.rem(seq + seqs - off, seqs)
             arrived(returned.at[slot_rows(source, e)], out_recv.at[e, off - 1])
     combined = upstream_ref[...].astype(F32)
-    for k, place in enumerate(places):
-        pick = (slot_at == place).astype(BF16)
-        combined = combined + weight_ref[:, k : k + 1] * dot(pick, returned[...])
-    resid_ref[...] = combined.astype(BF16)
+    for pair_weight, pick in zip(pair_weights, picks):
+        combined = combined + pair_weight * dot(pick, returned[...])
+    resid = combined.astype(BF16)
+    resid_ref[...] = resid
+
+    def index_of(s, r):
+        return s * reps + r
+
+    def resid_on(sub_off):
+        piece = index_of(lax.rem(sub + subs - sub_off, subs), rep)
+        for off in range(1, reps):
+            sent.append(
+                send(
+                    full.at[piece],
+                    full.at[piece],
+                    resr_send.at[off - 1, sub_off],
+                    resr_recv.at[off - 1, sub_off],
+                    {"rep": lax.rem(rep + off, reps)},
+                )
+            )
+
+    def project(piece):
+        cols = pl.ds(pl.multiple_of(piece * features, 128), features)
+        return dot_t(full[piece], proj[:, cols])
+
+    mine = index_of(sub, rep)
+    full[mine] = resid
+    for off in range(1, subs):
+        sent.append(
+            send(
+                full.at[mine],
+                full.at[mine],
+                resx_send.at[off - 1],
+                resx_recv.at[off - 1],
+                {"sub": lax.rem(sub + off, subs)},
+            )
+        )
+    resid_on(0)
+    total = project(mine)
+    for sub_off in range(subs):
+        from_sub = lax.rem(sub + subs - sub_off, subs)
+        if sub_off > 0:
+            piece = index_of(from_sub, rep)
+            arrived(full.at[piece], resx_recv.at[sub_off - 1])
+            resid_on(sub_off)
+            total = total + project(piece)
+        for off in range(1, reps):
+            piece = index_of(from_sub, lax.rem(rep + reps - off, reps))
+            arrived(full.at[piece], resr_recv.at[off - 1, sub_off])
+            total = total + project(piece)
+    head_grad[...] = total.astype(BF16)
+
+    for h in range(heads):
+        cols = of_head(h)
+        grad_state[h] = dot_0(query_ref[:, cols], head_grad[:, cols]).astype(BF16)
+    for off in range(1, seqs):
+        send_if(
+            seq >= off,
+            grad_state,
+            grad_state_in.at[off - 1],
+            after_send.at[off - 1],
+            after_recv.at[off - 1],
+            {"seq": lax.rem(seq + seqs - off, seqs)},
+        )
+
+    scaling = HEAD_DIM**-0.5
+    for h in range(heads):
+        cols = of_head(h)
+        q, o = query_ref[:, cols], head_grad[:, cols]
+        keys, values = keys_ext[:, cols], values_ext[:, cols]
+        softmax = probs[h]
+        centre = jnp.sum(o.astype(F32) * attended[:, cols], axis=1, keepdims=True)
+        score_grad = (softmax * (dot_t(o, values) - centre)).astype(BF16)
+        query_sum[:, cols] = dot(score_grad, keys) * scaling
+        key_ext = dot_0(score_grad, q) * scaling
+        value_ext = dot_0(softmax.astype(BF16), o)
+        key_sum[:, cols] = key_ext[window:]
+        value_sum[:, cols] = value_ext[window:]
+        carry[0, :, cols] = key_ext[:window].astype(BF16)
+        carry[1, :, cols] = value_ext[:window].astype(BF16)
+    send_if(
+        seq > 0,
+        carry,
+        carry_in,
+        carry_send.at[0],
+        carry_recv.at[0],
+        {"seq": lax.rem(seq + seqs - 1, seqs)},
+    )
+
+    linear = float(HEAD_DIM * rows * seqs) ** -0.5
+    causal = lax.broadcasted_iota(jnp.int32, (rows, rows), 0) >= lax.broadcasted_iota(
+        jnp.int32, (rows, rows), 1
+    )
+    for h in range(heads):
+        cols = of_head(h)
+        q, k, v, o = query_ref[:, cols], key_ref[:, cols], value_ref[:, cols], head_grad[:, cols]
+        value_dots = jnp.where(causal, dot_t(o, v), 0.0).astype(BF16)
+        lin_query = dot(value_dots, k) + dot_t(o, before[h].astype(BF16))
+        query_grad_ref[:, cols] = (query_sum[:, cols] + linear * lin_query).astype(BF16)
+        key_sum[:, cols] = key_sum[:, cols] + linear * dot_0(value_dots, q)
+        value_sum[:, cols] = value_sum[:, cols] + linear * dot_0(query_dots[h], o)
+
+    for off in range(1, seqs):
+
+        @pl.when(seq + off < seqs)
+        def _():
+            arrived(grad_state_in.at[off - 1], after_recv.at[off - 1])
+            after[...] = after[...] + grad_state_in[off - 1].astype(F32)
+
+    @pl.when(seq < seqs - 1)
+    def _():
+        arrived(carry_in, carry_recv.at[0])
+
+    for h in range(heads):
+        cols = of_head(h)
+        k, v = key_ref[:, cols], value_ref[:, cols]
+        later = after[h].astype(BF16)
+        key_total = key_sum[:, cols] + linear * dot_t(v, later)
+        value_total = value_sum[:, cols] + linear * dot(k, later)
+        low = rows - window
+        key_grad_ref[:low, cols] = key_total[:low].astype(BF16)
+        value_grad_ref[:low, cols] = value_total[:low].astype(BF16)
+        key_grad_ref[low:, cols] = (key_total[low:] + carry_in[0, :, cols].astype(F32)).astype(BF16)
+        value_grad_ref[low:, cols] = (
+            value_total[low:] + carry_in[1, :, cols].astype(F32)
+        ).astype(BF16)
     for copy in sent:
         copy.wait_send()
-
-
-def moe_backward(moe_input, upstream, expert_ids, router_weight, w_gate, w_up, w_down):
+    for cond, copy in sent_if:
+        pl.when(cond)(copy.wait_send)
+
+
+def local(
+    moe_input,
+    upstream,
+    expert_ids,
+    router_weight,
+    w_gate,
+    w_up,
+    w_down,
+    out_proj,
+    query,
+    key_in,
+    value,
+):
     rows, features = moe_input.shape
     seqs, subs, reps = lax.axis_size("seq"), lax.axis_size("sub"), lax.axis_size("rep")
     local_experts, _, hidden = w_gate.shape
@@ -387,11 +639,13 @@
     hbm = pl.BlockSpec(memory_space=pl.ANY)
     dma = pltpu.SemaphoreType.DMA
     n = local_experts
+    heads = features // HEAD_DIM
+    states = (heads, HEAD_DIM, HEAD_DIM)
     return pl.pallas_call(
-        functools.partial(moe_kernel, cap, tile),
-        out_shape=jax.ShapeDtypeStruct((rows, features), BF16),
-        in_specs=[vmem] * 5 + [hbm] * 3,
-        out_specs=vmem,
+        functools.partial(kernel, cap, tile),
+        out_shape=[jax.ShapeDtypeStruct((rows, features), BF16)] * 4,
+        in_specs=[vmem] * 7 + [hbm] * 4,
+        out_specs=[vmem] * 4,
         scratch_shapes=[
             pltpu.VMEM((experts * cap, 2 * features), BF16),
             pltpu.VMEM((n, block, 2 * features), BF16),
@@ -405,7 +659,26 @@
             pltpu.VMEM((n, block, 2 * hidden), BF16),
             pltpu.VMEM((n, block, features), BF16),
             pltpu.VMEM((experts * cap, features), BF16),
-            dma((3,)),
+            pltpu.VMEM(out_proj.shape, BF16),
+            pltpu.VMEM((rows + WINDOW, features), BF16),
+            pltpu.VMEM((rows + WINDOW, features), BF16),
+            pltpu.VMEM((heads, rows, rows + WINDOW), F32),
+            pltpu.VMEM((rows, features), F32),
+            pltpu.VMEM((heads, rows, rows), BF16),
+            pltpu.VMEM(states, BF16),
+            pltpu.VMEM((seqs - 1,) + states, BF16),
+            pltpu.VMEM(states, F32),
+            pltpu.VMEM(states, BF16),
+            pltpu.VMEM((seqs - 1,) + states, BF16),
+            pltpu.VMEM(states, F32),
+            pltpu.VMEM((subs * reps, rows, features), BF16),
+            pltpu.VMEM((rows, features), BF16),
+            pltpu.VMEM((rows, features), F32),
+            pltpu.VMEM((rows, features), F32),
+            pltpu.VMEM((rows, features), F32),
+            pltpu.VMEM((2, WINDOW, features), BF16),
+            pltpu.VMEM((2, WINDOW, features), BF16),
+            dma((4,)),
             dma((n,)),
             dma((n, seqs - 1)),
             dma((n, seqs - 1)),
@@ -419,158 +692,36 @@
             dma((n, reps - 1, subs)),
             dma((n, seqs - 1)),
             dma((n, seqs - 1)),
+            dma((2,)),
+            dma((2,)),
+            dma((seqs - 1,)),
+            dma((seqs - 1,)),
+            dma((seqs - 1,)),
+            dma((seqs - 1,)),
+            dma((subs - 1,)),
+            dma((subs - 1,)),
+            dma((reps - 1, subs)),
+            dma((reps - 1, subs)),
+            dma((1,)),
+            dma((1,)),
         ],
         compiler_params=pltpu.CompilerParams(
             collective_id=0, has_side_effects=True, vmem_limit_bytes=56 * 1024 * 1024
         ),
-        name="experts",
-    )(expert_ids, expert_ids.T, router_weight, moe_input, upstream, w_gate, w_up, w_down)
-
-
-def window_block(query_heads, keys_ext, values_ext, grad_heads, first_key):
-    row_count = query_heads.shape[0]
-    key_count = keys_ext.shape[0]
-    scaling = query_heads.shape[-1] ** (-0.5)
-    query_pos = lax.broadcasted_iota(jnp.int32, (row_count, key_count), 0)
-    key_pos = lax.broadcasted_iota(jnp.int32, (row_count, key_count), 1)
-    allowed = (key_pos > query_pos) & (key_pos <= query_pos + WINDOW) & (key_pos + first_key >= 0)
-    scores = (
-        jnp.einsum("ihd,jhd->hij", query_heads, keys_ext, preferred_element_type=jnp.float32)
-        * scaling
+        name="backward",
+    )(
+        expert_ids.T,
+        router_weight.T,
+        moe_input,
+        upstream,
+        query,
+        key_in,
+        value,
+        w_gate,
+        w_up,
+        w_down,
+        out_proj,
     )
-    scores = jnp.where(allowed[None], scores, -jnp.inf)
-    highest = jnp.max(scores, axis=2, keepdims=True)
-    weights = jnp.exp(scores - highest)
-    softmax_probs = weights / jnp.sum(weights, axis=2, keepdims=True)
-    probs_low = softmax_probs.astype(jnp.bfloat16)
-    attended = jnp.einsum("hij,jhe->ihe", probs_low, values_ext, preferred_element_type=jnp.float32)
-    centre = jnp.sum(grad_heads.astype(jnp.float32) * attended, axis=2)
-    prob_grad = jnp.einsum(
-        "ihe,jhe->hij", grad_heads, values_ext, preferred_element_type=jnp.float32
-    )
-    score_grad = (softmax_probs * (prob_grad - jnp.transpose(centre)[:, :, None])).astype(
-        jnp.bfloat16
-    )
-    win_query = (
-        jnp.einsum("hij,jhd->ihd", score_grad, keys_ext, preferred_element_type=jnp.float32)
-        * scaling
-    )
-    win_key = (
-        jnp.einsum("hij,ihd->jhd", score_grad, query_heads, preferred_element_type=jnp.float32)
-        * scaling
-    )
-    win_value = jnp.einsum(
-        "hij,ihe->jhe", probs_low, grad_heads, preferred_element_type=jnp.float32
-    )
-    return (win_query, win_key, win_value)
-
-
-def local(
-    moe_input,
-    upstream,
-    expert_ids,
-    router_weight,
-    w_gate,
-    w_up,
-    w_down,
-    out_proj,
-    query,
-    key_in,
-    value,
-):
-    row_count, features = moe_input.shape
-    seq_count = lax.axis_size("seq")
-    resid_grad = moe_backward(
-        moe_input, upstream, expert_ids, router_weight, w_gate, w_up, w_down
-    )
-    head_grad = lax.dot_general(
-        lax.all_gather(resid_grad, ("sub", "rep"), axis=1, tiled=True),
-        out_proj,
-        (((1,), (1,)), ((), ())),
-        preferred_element_type=jnp.float32,
-    ).astype(jnp.bfloat16)
-    head_dim = HEAD_DIM
-    local_heads = features // head_dim
-    head_shape = (row_count, local_heads, head_dim)
-    query_heads = query.reshape(head_shape)
-    key_heads = key_in.reshape(head_shape)
-    value_heads = value.reshape(head_shape)
-    grad_heads = head_grad.reshape(head_shape)
-    state_local = jnp.einsum(
-        "shd,she->hde", key_heads, value_heads, preferred_element_type=jnp.float32
-    )
-    grad_local = jnp.einsum(
-        "shd,she->hde", query_heads, grad_heads, preferred_element_type=jnp.float32
-    )
-    zero_state = jnp.zeros_like(state_local)
-    preceding_state = entering(state_local, "seq", add_single, zero_state, False)
-    gradient_following = entering(grad_local, "seq", add_single, zero_state, True)
-    causal_masking = (
-        lax.broadcasted_iota(jnp.int32, (row_count, row_count), 0)
-        >= lax.broadcasted_iota(jnp.int32, (row_count, row_count), 1)
-    )[None]
-    value_products = jnp.where(
-        causal_masking,
-        jnp.einsum("ihe,jhe->hij", grad_heads, value_heads, preferred_element_type=jnp.float32),
-        0.0,
-    ).astype(jnp.bfloat16)
-    query_products = jnp.where(
-        causal_masking,
-        jnp.einsum("ihd,jhd->hij", query_heads, key_heads, preferred_element_type=jnp.float32),
-        0.0,
-    ).astype(jnp.bfloat16)
-    linear_branch_scale = (head_dim * row_count * seq_count) ** (-0.5)
-    exact_precision = lax.Precision.HIGHEST
-    linear_query = linear_branch_scale * (
-        jnp.einsum(
-            "ihe,hde->ihd",
-            grad_heads.astype(jnp.float32),
-            preceding_state,
-            precision=exact_precision,
-        )
-        + jnp.einsum("hij,jhd->ihd", value_products, key_heads, preferred_element_type=jnp.float32)
-    )
-    lin_key = linear_branch_scale * (
-        jnp.einsum(
-            "jhe,hde->jhd",
-            value_heads.astype(jnp.float32),
-            gradient_following,
-            precision=exact_precision,
-        )
-        + jnp.einsum(
-            "hij,ihd->jhd", value_products, query_heads, preferred_element_type=jnp.float32
-        )
-    )
-    linear_value = linear_branch_scale * (
-        jnp.einsum(
-            "jhd,hde->jhe",
-            key_heads.astype(jnp.float32),
-            gradient_following,
-            precision=exact_precision,
-        )
-        + jnp.einsum("hij,ihe->jhe", query_products, grad_heads, preferred_element_type=jnp.float32)
-    )
-    window = WINDOW
-    first_row = lax.axis_index("seq") * row_count
-    halo_keys, halo_values = shifted(
-        (key_heads[row_count - window :], value_heads[row_count - window :]), "seq", 1
-    )
-    keys_ext = jnp.concatenate([halo_keys, key_heads], axis=0)
-    values_ext = jnp.concatenate([halo_values, value_heads], axis=0)
-    win_query, key_ext_grad, value_ext_grad = window_block(
-        query_heads, keys_ext, values_ext, grad_heads, first_row - window
-    )
-    carried_key, carried_value = (
-        shifted(key_ext_grad[:window].astype(jnp.bfloat16), "seq", -1).astype(jnp.float32),
-        shifted(value_ext_grad[:window].astype(jnp.bfloat16), "seq", -1).astype(jnp.float32),
-    )
-    padding = jnp.zeros((row_count - window, local_heads, head_dim), jnp.float32)
-    win_key = key_ext_grad[window:] + jnp.concatenate([padding, carried_key], axis=0)
-    win_value = value_ext_grad[window:] + jnp.concatenate([padding, carried_value], axis=0)
-    query_grad = (linear_query + win_query).astype(jnp.bfloat16).reshape(row_count, features)
-    key_grad = (lin_key + win_key).astype(jnp.bfloat16).reshape(row_count, features)
-    value_grad = (linear_value + win_value).astype(jnp.bfloat16).reshape(row_count, features)
-    return (resid_grad, query_grad, key_grad, value_grad)
 
 
 def solution(mesh):

time: 179 us -> 132 us (0.74)
  Pallas kernels: 80.8 us -> 125 us
  blocking collectives: 33.8 us -> 0 us
  matrix products: 18.7 us -> 0 us
  between operations: 14.3 us -> 0.65 us
  local copies, waits for them, and re-layouts: 15.3 us -> 5.76 us
  starting transfers between devices: 7.61 us -> 0 us
  other arithmetic: 5.4 us -> 0 us
  waiting for transfers between devices: 2.5 us -> 0 us
    pallas_call x1, Pallas kernels: 80.8 us -> 125 us  [local(): pl.pallas_call(functools.partial(kernel, cap, tile), out_shape=[jax.Shape...]
    all_gather x2 -> x0, blocking collectives: 33.8 us -> none  [entering(): everything = lax.all_gather(shard.astype(jnp.bfloat16), axis)]
    dot_general x15 -> x0, matrix products: 15.8 us -> none  [the longest x1 2.68 us: local(): lax.dot_general(lax.all_gather(resid_grad, ('sub', 'rep'), axis=1, tiled=...]
    ppermute x4 -> x0, starting transfers between devices: 7.57 us -> none  [shifted(): return lax.ppermute(block, axis, route)]
    select_n x8 -> x0, other arithmetic: 4.6 us -> none  [step(): return jnp.where(reached, new, before)]
    slice x6 -> x0, local copies, waits for them, and re-layouts: 4.25 us -> none  [the longest x1 1.73 us: local(): value_ext_grad[:window].astype(jnp.bfloat16)]
    reshape x4 -> x0, local copies, waits for them, and re-layouts: 3.97 us -> none  [the longest x1 1.89 us: local(): query_heads = query.reshape(head_shape)]
    sub x1 -> x0, matrix products: 2.85 us -> none  [window_block(): weights = jnp.exp(scores - highest)]
  transfers between devices with their start and end apart: 5 -> 0, of which waited for: 1 -> 0; matrix products, arithmetic and copies ran while one was open for 14% -> 0% of each run, Pallas kernels for 0% -> 0%
where the time goes in v2:
time: 132 us; the launch traced here: 131 us
  Pallas kernels  125 us (95%)
  local copies, waits for them, and re-layouts  5.76 us (4%)
    pallas_call x1, Pallas kernels, local(): pl.pallas_call(functools.partial(kernel, cap, tile), out_shape=[jax.Shape...  125 us
    unnamed x6, local copies, waits for them, and re-layouts  5.76 us

profile of v2, /device:TPU:0, one launch (start us, length us, event | category | flops | bytes accessed | tf_op | source)
XLA Modules:
  0.0 131.4 jit_solution(13645869699848502811)
XLA Ops:
  0.6 125.0 %backward.1 = (bf16[256,512]{1,0:T(8,128)(2,1)}, bf16[256,512]{1,0:T(8,128)(2,1)}, bf16[256,512]{1,0:T(8,128)(2,1)}, bf16[256,512]{1,0:T(8,128)(2,1)}) custom-call(s32[2,256]{1,0:T(2,128)} %bitcast.2, f32[2,256]{1,0:T(2,128)} %bitcast.3, bf16[256,512]{1,0:T(8,128)(2,1)} %input_ref.1, bf16[256,512]{1,0:T(8,128)(2,1)} %upstream_ref.1, ...), custom_call_target="tpu_custom_call" | custom-call | tf_op jit(solution)/shard_map/backward/pallas_call | solution.py:644
  125.7 0.0 copy-start
  125.7 1.7 %copy.19 = bf16[256,512]{1,0:T(8,128)(2,1)} copy(bf16[256,512]{1,0:T(8,128)(2,1)} %get-tuple-element.8) | data formatting | bytes 524288
  127.4 1.7 %copy.20 = bf16[256,512]{1,0:T(8,128)(2,1)} copy(bf16[256,512]{1,0:T(8,128)(2,1)} %get-tuple-element.9) | data formatting | bytes 524288
  129.1 1.7 %copy.21 = bf16[256,512]{1,0:T(8,128)(2,1)} copy(bf16[256,512]{1,0:T(8,128)(2,1)} %get-tuple-element.10) | data formatting | bytes 524288
  130.7 0.0 copy-done
  130.7 0.7 copy.22
Async XLA Ops:
  125.7 5.1 %copy-start = (bf16[256,512]{1,0:T(8,128)(2,1)S(1)}, bf16[256,512]{1,0:T(8,128)(2,1)}, u32[]{:S(2)}) copy-start(bf16[256,512]{1,0:T(8,128)(2,1)} %get-tuple-element.11) | copy-start | bytes 786436

commit v3 on v2

--- a/solution.py
+++ b/solution.py
@@ -9,6 +9,7 @@
 
 HEAD_DIM = 128
 WINDOW = 128
+SPLITS = 2
 MESH = pl.DeviceIdType.MESH
 F32 = jnp.float32
 BF16 = jnp.bfloat16
@@ -59,17 +60,29 @@
     pl.semaphore_wait(barrier, count)
 
 
-def slots_of(ids_t, cap, expert_count):
-    chosen, rows = ids_t.shape
-    experts = lax.broadcasted_iota(jnp.int32, (expert_count, rows), 0)
-    named = [(experts == ids_t[k : k + 1, :]).astype(F32) for k in range(chosen)]
+def slots_of(ids, local_experts, splits, chunk_cap, seqs):
+    chosen, rows = ids.shape
+    block = seqs * chunk_cap
+    experts = lax.broadcasted_iota(jnp.int32, (local_experts * seqs, rows), 0)
+    named = [(experts == ids[k : k + 1, :]).astype(F32) for k in range(chosen)]
     earlier = (
         lax.broadcasted_iota(jnp.int32, (rows, rows), 0)
         < lax.broadcasted_iota(jnp.int32, (rows, rows), 1)
     ).astype(BF16)
     rank = dot(sum(named).astype(BF16), earlier)
-    first = experts.astype(F32) * cap + rank
-    return [jnp.sum(n * first, axis=0, keepdims=True) for n in named]
+    owner = jnp.zeros(experts.shape, F32)
+    for i in range(1, seqs):
+        owner = owner + (experts >= i * local_experts).astype(F32)
+    local = experts.astype(F32) - owner * local_experts
+    first = local * (splits * block) + owner * chunk_cap
+    places = []
+    for n in named:
+        own_rank = jnp.sum(n * rank, axis=0, keepdims=True)
+        place = jnp.sum(n * first, axis=0, keepdims=True) + own_rank
+        for i in range(1, splits):
+            place = place + (own_rank >= i * chunk_cap).astype(F32) * (block - chunk_cap)
+        places.append(place)
+    return places
 
 
 def as_column(line):
@@ -86,6 +99,7 @@
 
 def kernel(
     cap,
+    splits,
     tile,
     ids_ref,
     weight_ref,
@@ -166,6 +180,8 @@
     experts = local_experts * seqs
     half_rows = half.shape[2]
     piece_rows = half_rows // subs
+    block = seqs * cap
+    chunks = local_experts * splits
     sent = []
     sent_if = []
     rows = ids_ref.shape[1]
@@ -197,8 +213,8 @@
     for copy in weight_copies:
         copy.start()
 
-    def slot_rows(owner, e):
-        return pl.ds(pl.multiple_of((owner * local_experts + e) * cap, 16), cap)
+    def slot_rows(owner, c):
+        return pl.ds(pl.multiple_of(c * block + owner * cap, 16), cap)
 
     def source_rows(source):
         return pl.ds(pl.multiple_of(source * cap, 16), cap)
@@ -212,44 +228,41 @@
     def rows_of(r, s):
         return pl.ds(pl.multiple_of(r * half_rows + s * piece_rows, 16), piece_rows)
 
-    places = slots_of(ids_ref[...], cap, experts)
-    slot_count = experts * cap
-    slot_at = lax.broadcasted_iota(jnp.int32, (slot_count, places[0].shape[1]), 0).astype(F32)
-    pick = jnp.zeros(slot_at.shape, F32)
-    for place in places:
-        pick = pick + (slot_at == place).astype(F32)
-    pick = pick.astype(BF16)
-    slots[:, :features] = dot(pick, input_ref[...]).astype(BF16)
-    slots[:, features:] = dot(pick, upstream_ref[...]).astype(BF16)
-
-    greet(("seq", "sub", "rep"))
-
-    own = []
-    for e in range(local_experts):
-        copy = pltpu.make_async_copy(
-            slots.at[slot_rows(seq, e)], received.at[e, source_rows(seq)], own_sem.at[e]
+    places = slots_of(ids_ref[...], local_experts, splits, cap, seqs)
+
+    def fill(c):
+        slot_at = lax.broadcasted_iota(jnp.int32, (block, rows), 0).astype(F32) + float(c * block)
+        pick = jnp.zeros(slot_at.shape, F32)
+        for place in places:
+            pick = pick + (slot_at == place).astype(F32)
+        pick = pick.astype(BF16)
+        slots[c * block : (c + 1) * block, :features] = dot(pick, input_ref[...]).astype(BF16)
+        slots[c * block : (c + 1) * block, features:] = dot(pick, upstream_ref[...]).astype(BF16)
+
+    own = [None] * chunks
+    batches = [None] * chunks
+
+    def start(c):
+        own[c] = pltpu.make_async_copy(
+            slots.at[slot_rows(seq, c)], received.at[c, source_rows(seq)], own_sem.at[c]
         )
-        copy.start()
-        own.append(copy)
-        batch = []
+        own[c].start()
+        batches[c] = []
         for off in range(1, seqs):
             target = lax.rem(seq + off, seqs)
-            batch.append(
+            batches[c].append(
                 send(
-                    slots.at[slot_rows(target, e)],
-                    received.at[e, source_rows(seq)],
-                    in_send.at[e, off - 1],
-                    in_recv.at[e, off - 1],
+                    slots.at[slot_rows(target, c)],
+                    received.at[c, source_rows(seq)],
+                    in_send.at[c, off - 1],
+                    in_recv.at[c, off - 1],
                     {"seq": target},
                 )
             )
-        if e < local_experts - 1:
-            for copy in batch:
-                copy.wait_send()
-        else:
-            sent.extend(batch)
-    for copy in weight_copies:
-        copy.wait()
+
+    def left(c):
+        for copy in batches[c]:
+            copy.wait_send()
 
     def first_products(e):
         own[e].wait()
@@ -262,11 +275,11 @@
             def _(j):
                 cols = pl.ds(pl.multiple_of(j * tile, tile), tile)
                 if a == 0:
-                    got = dot(received[e, :, :features], w_gate[e, :, cols])
+                    got = dot(received[e, :, :features], w_gate[e // splits, :, cols])
                 elif a == 1:
-                    got = dot(received[e, :, :features], w_up[e, :, cols])
+                    got = dot(received[e, :, :features], w_up[e // splits, :, cols])
                 else:
-                    got = dot_t(received[e, :, features:], w_down[e, cols, :])
+                    got = dot_t(received[e, :, features:], w_down[e // splits, cols, :])
                 part[e, a, :, cols] = got.astype(BF16)
 
             for off in range(1, reps):
@@ -358,8 +371,8 @@
         @pl.loop(0, features // step)
         def _(j):
             cols = pl.ds(pl.multiple_of(j * step, step), step)
-            got = dot_t(grads[e, :, :hidden], w_gate[e, cols, :])
-            got = got + dot_t(grads[e, :, hidden:], w_up[e, cols, :])
+            got = dot_t(grads[e, :, :hidden], w_gate[e // splits, cols, :])
+            got = got + dot_t(grads[e, :, hidden:], w_up[e // splits, cols, :])
             out[e, :, cols] = got.astype(BF16)
 
         copy = pltpu.make_async_copy(
@@ -403,7 +416,7 @@
         before[...] = jnp.zeros(before.shape, F32)
         after[...] = jnp.zeros(after.shape, F32)
 
-    def send_own_parts():
+    def send_halos():
         tail = pl.ds(rows - window, window)
         for n, (src, dst) in enumerate(((key_ref, keys_ext), (value_ref, values_ext))):
             send_if(
@@ -414,6 +427,8 @@
                 halo_recv.at[n],
                 {"seq": lax.rem(seq + 1, seqs)},
             )
+
+    def send_states():
         for off in range(1, seqs):
             send_if(
                 seq + off < seqs,
@@ -455,31 +470,45 @@
                 arrived(state_in.at[off - 1], state_recv.at[off - 1])
                 before[...] = before[...] + state_in[off - 1].astype(F32)
 
+    fill(0)
+    greet(("seq", "sub", "rep"))
+    start(0)
+    for c in range(1, chunks):
+        fill(c)
     own_parts()
-    for e in range(local_experts):
-        first_products(e)
-        if e == local_experts - 1:
-            send_own_parts()
-        if e > 0:
-            second_products(e - 1)
-        if e == local_experts - 1:
-            window_probs()
-            states_before()
-        gate(e)
-    second_products(local_experts - 1)
-
     columns = [as_column(place) for place in places]
     pair_weights = [as_column(weight_ref[k : k + 1, :]) for k in range(len(places))]
-    slot_at = lax.broadcasted_iota(jnp.int32, (rows, slot_count), 1).astype(F32)
-    picks = [(slot_at == column).astype(BF16) for column in columns]
-    for e in range(local_experts):
-        own[e].wait()
+    left(0)
+    if chunks > 1:
+        start(1)
+    for copy in weight_copies:
+        copy.wait()
+    for c in range(chunks):
+        first_products(c)
+        if c + 1 < chunks:
+            left(c + 1)
+        if c + 2 < chunks:
+            start(c + 2)
+        if c == chunks - 1:
+            send_halos()
+        if c > 0:
+            second_products(c - 1)
+        gate(c)
+    second_products(chunks - 1)
+    window_probs()
+
+    combined = upstream_ref[...].astype(F32)
+    for c in range(chunks):
+        slot_at = lax.broadcasted_iota(jnp.int32, (rows, block), 1).astype(F32) + float(c * block)
+        own[c].wait()
         for off in range(1, seqs):
             source = lax.rem(seq + seqs - off, seqs)
-            arrived(returned.at[slot_rows(source, e)], out_recv.at[e, off - 1])
-    combined = upstream_ref[...].astype(F32)
-    for pair_weight, pick in zip(pair_weights, picks):
-        combined = combined + pair_weight * dot(pick, returned[...])
+            arrived(returned.at[slot_rows(source, c)], out_recv.at[c, off - 1])
+        for pair_weight, column in zip(pair_weights, columns):
+            pick = (slot_at == column).astype(BF16)
+            combined = combined + pair_weight * dot(
+                pick, returned[c * block : (c + 1) * block, :]
+            )
     resid = combined.astype(BF16)
     resid_ref[...] = resid
 
@@ -516,6 +545,7 @@
             )
         )
     resid_on(0)
+    send_states()
     total = project(mine)
     for sub_off in range(subs):
         from_sub = lax.rem(sub + subs - sub_off, subs)
@@ -575,11 +605,15 @@
         cols = of_head(h)
         q, k, v, o = query_ref[:, cols], key_ref[:, cols], value_ref[:, cols], head_grad[:, cols]
         value_dots = jnp.where(causal, dot_t(o, v), 0.0).astype(BF16)
-        lin_query = dot(value_dots, k) + dot_t(o, before[h].astype(BF16))
-        query_grad_ref[:, cols] = (query_sum[:, cols] + linear * lin_query).astype(BF16)
+        query_sum[:, cols] = query_sum[:, cols] + linear * dot(value_dots, k)
         key_sum[:, cols] = key_sum[:, cols] + linear * dot_0(value_dots, q)
         value_sum[:, cols] = value_sum[:, cols] + linear * dot_0(query_dots[h], o)
 
+    states_before()
+    for h in range(heads):
+        cols = of_head(h)
+        lin_query = dot_t(head_grad[:, cols], before[h].astype(BF16))
+        query_grad_ref[:, cols] = (query_sum[:, cols] + linear * lin_query).astype(BF16)
     for off in range(1, seqs):
 
         @pl.when(seq + off < seqs)
@@ -631,6 +665,11 @@
     cap = -(-cap // 16) * 16
     while seqs * cap % (16 * subs * reps):
         cap += 16
+    splits = SPLITS
+    while cap % (16 * splits) or seqs * cap // splits % (16 * subs * reps):
+        splits -= 1
+    slot_count = experts * cap
+    cap = cap // splits
     tile = 256 if hidden % 256 == 0 else hidden
     block = seqs * cap
     half_rows = block // reps
@@ -638,16 +677,16 @@
     vmem = pl.BlockSpec(memory_space=pltpu.VMEM)
     hbm = pl.BlockSpec(memory_space=pl.ANY)
     dma = pltpu.SemaphoreType.DMA
-    n = local_experts
+    n = local_experts * splits
     heads = features // HEAD_DIM
     states = (heads, HEAD_DIM, HEAD_DIM)
-    return pl.pallas_call(
-        functools.partial(kernel, cap, tile),
+    results = pl.pallas_call(
+        functools.partial(kernel, cap, splits, tile),
         out_shape=[jax.ShapeDtypeStruct((rows, features), BF16)] * 4,
         in_specs=[vmem] * 7 + [hbm] * 4,
         out_specs=[vmem] * 4,
         scratch_shapes=[
-            pltpu.VMEM((experts * cap, 2 * features), BF16),
+            pltpu.VMEM((slot_count, 2 * features), BF16),
             pltpu.VMEM((n, block, 2 * features), BF16),
             pltpu.VMEM(w_gate.shape, BF16),
             pltpu.VMEM(w_up.shape, BF16),
@@ -658,7 +697,7 @@
             pltpu.VMEM((n, 3, subs - 1, piece_rows, hidden), BF16),
             pltpu.VMEM((n, block, 2 * hidden), BF16),
             pltpu.VMEM((n, block, features), BF16),
-            pltpu.VMEM((experts * cap, features), BF16),
+            pltpu.VMEM((slot_count, features), BF16),
             pltpu.VMEM(out_proj.shape, BF16),
             pltpu.VMEM((rows + WINDOW, features), BF16),
             pltpu.VMEM((rows + WINDOW, features), BF16),
@@ -722,6 +761,23 @@
         w_down,
         out_proj,
     )
+    return pl.pallas_call(
+        place_kernel,
+        out_shape=[jax.ShapeDtypeStruct((rows, features), BF16)] * 4,
+        in_specs=[hbm] * 4,
+        out_specs=[hbm] * 4,
+        scratch_shapes=[dma((4,))],
+        name="place",
+    )(*results)
+
+
+def place_kernel(*refs):
+    sems = refs[-1]
+    copies = [pltpu.make_async_copy(refs[i], refs[4 + i], sems.at[i]) for i in range(4)]
+    for copy in copies:
+        copy.start()
+    for copy in copies:
+        copy.wait()
 
 
 def solution(mesh):

time: 132 us -> 134 us (1.015); the launches traced: 131 us -> 132 us
  Pallas kernels: 125 us -> 131 us
  local copies, waits for them, and re-layouts: 5.76 us -> 0 us
    pallas_call x1 -> x2, Pallas kernels: 125 us -> 131 us  [the longest x1 98 us: local(): pl.pallas_call(functools.partial(kernel, cap, splits, tile), out_shape=[j...]
    unnamed x6 -> x0, local copies, waits for them, and re-layouts: 5.76 us -> none
where the time goes in v3:
time: 134 us; the launch traced here: 132 us
  Pallas kernels  131 us (98%)
    pallas_call x1, Pallas kernels, local(): pl.pallas_call(functools.partial(kernel, cap, splits, tile), out_shape=[j...  98 us
    pallas_call x1, Pallas kernels, local(): pl.pallas_call(place_kernel, out_shape=[jax.ShapeDtypeStruct((rows, featu...  32.9 us

profile of v3, /device:TPU:0, one launch (start us, length us, event | category | flops | bytes accessed | tf_op | source)
XLA Modules:
  0.0 131.6 jit_solution(5230038516947259296)
XLA Ops:
  0.6 98.0 %backward.1 = (bf16[256,512]{1,0:T(8,128)(2,1)}, bf16[256,512]{1,0:T(8,128)(2,1)}, bf16[256,512]{1,0:T(8,128)(2,1)}, bf16[256,512]{1,0:T(8,128)(2,1)}) custom-call(s32[2,256]{1,0:T(2,128)} %bitcast.2, f32[2,256]{1,0:T(2,128)} %bitcast.3, bf16[256,512]{1,0:T(8,128)(2,1)} %input_ref.1, bf16[256,512]{1,0:T(8,128)(2,1)} %upstream_ref.1, ...), custom_call_target="tpu_custom_call" | custom-call | tf_op jit(solution)/shard_map/backward/pallas_call | solution.py:683
  98.7 32.9 %place.1 = (bf16[256,512]{1,0:T(8,128)(2,1)}, bf16[256,512]{1,0:T(8,128)(2,1)}, bf16[256,512]{1,0:T(8,128)(2,1)}, bf16[256,512]{1,0:T(8,128)(2,1)}) custom-call(bf16[256,512]{1,0:T(8,128)(2,1)} %get-tuple-element.8.refs_0_, bf16[256,512]{1,0:T(8,128)(2,1)} %get-tuple-element.9.refs_1_, bf16[256,512]{1,0:T(8,128)(2,1)} %get-tuple-element.10.refs_2_, ...), custom_call_target="tpu_custom_call" | custom-call | tf_op jit(solution)/shard_map/place/pallas_call | solution.py:764

commit v4 on v3

--- a/solution.py
+++ b/solution.py
@@ -9,7 +9,7 @@
 
 HEAD_DIM = 128
 WINDOW = 128
-SPLITS = 2
+SPLITS = 3
 MESH = pl.DeviceIdType.MESH
 F32 = jnp.float32
 BF16 = jnp.bfloat16
@@ -764,20 +764,15 @@
     return pl.pallas_call(
         place_kernel,
         out_shape=[jax.ShapeDtypeStruct((rows, features), BF16)] * 4,
-        in_specs=[hbm] * 4,
-        out_specs=[hbm] * 4,
-        scratch_shapes=[dma((4,))],
+        in_specs=[vmem] * 4,
+        out_specs=[vmem] * 4,
         name="place",
     )(*results)
 
 
 def place_kernel(*refs):
-    sems = refs[-1]
-    copies = [pltpu.make_async_copy(refs[i], refs[4 + i], sems.at[i]) for i in range(4)]
-    for copy in copies:
-        copy.start()
-    for copy in copies:
-        copy.wait()
+    for src, dst in zip(refs[:4], refs[4:]):
+        dst[...] = src[...]
 
 
 def solution(mesh):

time: 134 us -> 104 us (0.78)
  the two profiles are of different devices: /device:TPU:0 before, /device:TPU:11 now
where the time goes in v4:
time: 104 us
  Pallas kernels  103 us (99%)
    pallas_call x1, Pallas kernels, local(): pl.pallas_call(functools.partial(kernel, cap, splits, tile), out_shape=[j...  101 us
    pallas_call x1, Pallas kernels, local(): pl.pallas_call(place_kernel, out_shape=[jax.ShapeDtypeStruct((rows, featu...  2.17 us

profile of v4, /device:TPU:11, one launch (start us, length us, event | category | flops | bytes accessed | tf_op | source)
XLA Modules:
  0.0 104.1 jit_solution(4651065280452293705)
XLA Ops:
  0.6 101.3 %backward.1 = (bf16[256,512]{1,0:T(8,128)(2,1)}, bf16[256,512]{1,0:T(8,128)(2,1)}, bf16[256,512]{1,0:T(8,128)(2,1)}, bf16[256,512]{1,0:T(8,128)(2,1)}) custom-call(s32[2,256]{1,0:T(2,128)} %bitcast.2, f32[2,256]{1,0:T(2,128)} %bitcast.3, bf16[256,512]{1,0:T(8,128)(2,1)} %input_ref.1, bf16[256,512]{1,0:T(8,128)(2,1)} %upstream_ref.1, ...), custom_call_target="tpu_custom_call" | custom-call | tf_op jit(solution)/shard_map/backward/pallas_call | solution.py:683
  101.9 2.2 %place.1 = (bf16[256,512]{1,0:T(8,128)(2,1)}, bf16[256,512]{1,0:T(8,128)(2,1)}, bf16[256,512]{1,0:T(8,128)(2,1)}, bf16[256,512]{1,0:T(8,128)(2,1)}) custom-call(bf16[256,512]{1,0:T(8,128)(2,1)} %get-tuple-element.8.refs_0_, bf16[256,512]{1,0:T(8,128)(2,1)} %get-tuple-element.9.refs_1_, bf16[256,512]{1,0:T(8,128)(2,1)} %get-tuple-element.10.refs_2_, ...), custom_call_target="tpu_custom_call" | custom-call | tf_op jit(solution)/shard_map/place/pallas_call | solution.py:764

commit v5 on v4

--- a/solution.py
+++ b/solution.py
@@ -269,6 +269,8 @@
         for off in range(1, seqs):
             source = lax.rem(seq + seqs - off, seqs)
             arrived(received.at[e, source_rows(source)], in_recv.at[e, off - 1])
+        if e + 2 < chunks:
+            start(e + 2)
         for a in range(3):
 
             @pl.loop(0, hidden // tile)
@@ -293,6 +295,8 @@
                         {"rep": target},
                     )
                 )
+
+    def chip_sums(e):
         for a in range(3):
             for off in range(1, reps):
                 arrived(rep_in.at[e, a, off - 1], rep_recv.at[e, a, off - 1])
@@ -352,13 +356,15 @@
                 )
             )
 
-    def second_products(e):
+    def forward(e):
         for sub_off in range(1, subs):
             arrived(
                 grads.at[e, rows_of(rep, lax.rem(sub + subs - sub_off, subs))],
                 agx_recv.at[e, sub_off - 1],
             )
             pass_on(e, sub_off)
+
+    def second_products(e):
         for off in range(1, reps):
             for sub_off in range(subs):
                 piece = rows_of(
@@ -483,18 +489,21 @@
         start(1)
     for copy in weight_copies:
         copy.wait()
-    for c in range(chunks):
-        first_products(c)
-        if c + 1 < chunks:
-            left(c + 1)
-        if c + 2 < chunks:
-            start(c + 2)
+    for c in range(chunks + 2):
+        if 2 <= c:
+            forward(c - 2)
+        if c < chunks:
+            first_products(c)
         if c == chunks - 1:
             send_halos()
-        if c > 0:
-            second_products(c - 1)
-        gate(c)
-    second_products(chunks - 1)
+        if 1 <= c <= chunks:
+            gate(c - 1)
+        if c < chunks:
+            chip_sums(c)
+        if 2 <= c:
+            second_products(c - 2)
+    for batch in batches[1:]:
+        sent.extend(batch)
     window_probs()
 
     combined = upstream_ref[...].astype(F32)

time: 104 us -> 101 us (0.971)
  the two profiles are of different devices: /device:TPU:11 before, /device:TPU:0 now
where the time goes in v5:
time: 101 us; the launch traced here: 99.7 us
  Pallas kernels  99 us (98%)
    pallas_call x1, Pallas kernels, local(): pl.pallas_call(functools.partial(kernel, cap, splits, tile), out_shape=[j...  96.9 us
    pallas_call x1, Pallas kernels, local(): pl.pallas_call(place_kernel, out_shape=[jax.ShapeDtypeStruct((rows, featu...  2.17 us

profile of v5, /device:TPU:0, one launch (start us, length us, event | category | flops | bytes accessed | tf_op | source)
XLA Modules:
  0.0 99.7 jit_solution(8802406833715941775)
XLA Ops:
  0.6 96.9 %backward.1 = (bf16[256,512]{1,0:T(8,128)(2,1)}, bf16[256,512]{1,0:T(8,128)(2,1)}, bf16[256,512]{1,0:T(8,128)(2,1)}, bf16[256,512]{1,0:T(8,128)(2,1)}) custom-call(s32[2,256]{1,0:T(2,128)} %bitcast.2, f32[2,256]{1,0:T(2,128)} %bitcast.3, bf16[256,512]{1,0:T(8,128)(2,1)} %input_ref.1, bf16[256,512]{1,0:T(8,128)(2,1)} %upstream_ref.1, ...), custom_call_target="tpu_custom_call" | custom-call | tf_op jit(solution)/shard_map/backward/pallas_call | solution.py:692
  97.5 2.2 %place.1 = (bf16[256,512]{1,0:T(8,128)(2,1)}, bf16[256,512]{1,0:T(8,128)(2,1)}, bf16[256,512]{1,0:T(8,128)(2,1)}, bf16[256,512]{1,0:T(8,128)(2,1)}) custom-call(bf16[256,512]{1,0:T(8,128)(2,1)} %get-tuple-element.8.refs_0_, bf16[256,512]{1,0:T(8,128)(2,1)} %get-tuple-element.9.refs_1_, bf16[256,512]{1,0:T(8,128)(2,1)} %get-tuple-element.10.refs_2_, ...), custom_call_target="tpu_custom_call" | custom-call | tf_op jit(solution)/shard_map/place/pallas_call | solution.py:773

commit v6 on v5

--- a/solution.py
+++ b/solution.py
@@ -572,18 +572,42 @@
     for h in range(heads):
         cols = of_head(h)
         grad_state[h] = dot_0(query_ref[:, cols], head_grad[:, cols]).astype(BF16)
-    for off in range(1, seqs):
-        send_if(
-            seq >= off,
-            grad_state,
-            grad_state_in.at[off - 1],
-            after_send.at[off - 1],
-            after_recv.at[off - 1],
-            {"seq": lax.rem(seq + seqs - off, seqs)},
+    parts = 2 if heads % 2 == 0 else 1
+    passes = []
+    for p in range(parts):
+        some = pl.ds(p * (heads // parts), heads // parts)
+        passes.append(
+            pltpu.make_async_remote_copy(
+                src_ref=grad_state.at[some],
+                dst_ref=grad_state_in.at[some],
+                send_sem=after_send.at[p],
+                recv_sem=after_recv.at[p],
+                device_id={"seq": lax.rem(seq + seqs - 1, seqs)},
+                device_id_type=MESH,
+            )
         )
+        sent_if.append((seq > 0, passes[p]))
+
+    def relay():
+        for p in range(parts):
+            some = pl.ds(p * (heads // parts), heads // parts)
+
+            @pl.when(seq < seqs - 1)
+            def _():
+                arrived(grad_state_in.at[some], after_recv.at[p])
+                later = grad_state_in[some].astype(F32)
+                after[some] = later
+                grad_state[some] = (grad_state[some].astype(F32) + later).astype(BF16)
+
+            pl.when(seq > 0)(passes[p].start)
 
     scaling = HEAD_DIM**-0.5
-    for h in range(heads):
+    linear = float(HEAD_DIM * rows * seqs) ** -0.5
+    causal = lax.broadcasted_iota(jnp.int32, (rows, rows), 0) >= lax.broadcasted_iota(
+        jnp.int32, (rows, rows), 1
+    )
+
+    def window_part(h):
         cols = of_head(h)
         q, o = query_ref[:, cols], head_grad[:, cols]
         keys, values = keys_ext[:, cols], values_ext[:, cols]
@@ -597,20 +621,17 @@
         value_sum[:, cols] = value_ext[window:]
         carry[0, :, cols] = key_ext[:window].astype(BF16)
         carry[1, :, cols] = value_ext[:window].astype(BF16)
-    send_if(
-        seq > 0,
-        carry,
-        carry_in,
-        carry_send.at[0],
-        carry_recv.at[0],
-        {"seq": lax.rem(seq + seqs - 1, seqs)},
-    )
-
-    linear = float(HEAD_DIM * rows * seqs) ** -0.5
-    causal = lax.broadcasted_iota(jnp.int32, (rows, rows), 0) >= lax.broadcasted_iota(
-        jnp.int32, (rows, rows), 1
-    )
-    for h in range(heads):
+        if h == heads - 1:
+            send_if(
+                seq > 0,
+                carry,
+                carry_in,
+                carry_send.at[0],
+                carry_recv.at[0],
+                {"seq": lax.rem(seq + seqs - 1, seqs)},
+            )
+
+    def linear_part(h):
         cols = of_head(h)
         q, k, v, o = query_ref[:, cols], key_ref[:, cols], value_ref[:, cols], head_grad[:, cols]
         value_dots = jnp.where(causal, dot_t(o, v), 0.0).astype(BF16)
@@ -618,18 +639,18 @@
         key_sum[:, cols] = key_sum[:, cols] + linear * dot_0(value_dots, q)
         value_sum[:, cols] = value_sum[:, cols] + linear * dot_0(query_dots[h], o)
 
+    units = [functools.partial(window_part, h) for h in range(heads)]
+    units += [functools.partial(linear_part, h) for h in range(heads)]
+    turn = jnp.minimum(2 * (seqs - 1 - seq), len(units) - 1)
+    for u, unit in enumerate(units):
+        pl.when(turn == u)(relay)
+        unit()
+
     states_before()
     for h in range(heads):
         cols = of_head(h)
         lin_query = dot_t(head_grad[:, cols], before[h].astype(BF16))
         query_grad_ref[:, cols] = (query_sum[:, cols] + linear * lin_query).astype(BF16)
-    for off in range(1, seqs):
-
-        @pl.when(seq + off < seqs)
-        def _():
-            arrived(grad_state_in.at[off - 1], after_recv.at[off - 1])
-            after[...] = after[...] + grad_state_in[off - 1].astype(F32)
-
     @pl.when(seq < seqs - 1)
     def _():
         arrived(carry_in, carry_recv.at[0])
@@ -717,7 +738,7 @@
             pltpu.VMEM((seqs - 1,) + states, BF16),
             pltpu.VMEM(states, F32),
             pltpu.VMEM(states, BF16),
-            pltpu.VMEM((seqs - 1,) + states, BF16),
+            pltpu.VMEM(states, BF16),
             pltpu.VMEM(states, F32),
             pltpu.VMEM((subs * reps, rows, features), BF16),
             pltpu.VMEM((rows, features), BF16),
@@ -744,8 +765,8 @@
             dma((2,)),
             dma((seqs - 1,)),
             dma((seqs - 1,)),
-            dma((seqs - 1,)),
-            dma((seqs - 1,)),
+            dma((2,)),
+            dma((2,)),
             dma((subs - 1,)),
             dma((subs - 1,)),
             dma((reps - 1, subs)),

time: 101 us -> 97.5 us (0.965); the launches traced: 99.7 us -> 97.4 us
  Pallas kernels: 99 us -> 96.7 us
    pallas_call x1, Pallas kernels: 96.9 us -> 94.6 us  [local(): pl.pallas_call(functools.partial(kernel, cap, splits, tile), out_shape=[j...]
where the time goes in v6:
time: 97.5 us; the launch traced here: 97.4 us
  Pallas kernels  96.7 us (99%)
    pallas_call x1, Pallas kernels, local(): pl.pallas_call(functools.partial(kernel, cap, splits, tile), out_shape=[j...  94.6 us
    pallas_call x1, Pallas kernels, local(): pl.pallas_call(place_kernel, out_shape=[jax.ShapeDtypeStruct((rows, featu...  2.17 us

profile of v6, /device:TPU:0, one launch (start us, length us, event | category | flops | bytes accessed | tf_op | source)
XLA Modules:
  0.0 97.4 jit_solution(1301805740503596469)
XLA Ops:
  0.6 94.6 %backward.1 = (bf16[256,512]{1,0:T(8,128)(2,1)}, bf16[256,512]{1,0:T(8,128)(2,1)}, bf16[256,512]{1,0:T(8,128)(2,1)}, bf16[256,512]{1,0:T(8,128)(2,1)}) custom-call(s32[2,256]{1,0:T(2,128)} %bitcast.2, f32[2,256]{1,0:T(2,128)} %bitcast.3, bf16[256,512]{1,0:T(8,128)(2,1)} %input_ref.1, bf16[256,512]{1,0:T(8,128)(2,1)} %upstream_ref.1, ...), custom_call_target="tpu_custom_call" | custom-call | tf_op jit(solution)/shard_map/backward/pallas_call | solution.py:713
  95.2 2.2 %place.1 = (bf16[256,512]{1,0:T(8,128)(2,1)}, bf16[256,512]{1,0:T(8,128)(2,1)}, bf16[256,512]{1,0:T(8,128)(2,1)}, bf16[256,512]{1,0:T(8,128)(2,1)}) custom-call(bf16[256,512]{1,0:T(8,128)(2,1)} %get-tuple-element.8.refs_0_, bf16[256,512]{1,0:T(8,128)(2,1)} %get-tuple-element.9.refs_1_, bf16[256,512]{1,0:T(8,128)(2,1)} %get-tuple-element.10.refs_2_, ...), custom_call_target="tpu_custom_call" | custom-call | tf_op jit(solution)/shard_map/place/pallas_call | solution.py:794
